TPU v7x, 768 devices: a whole 4x8x12 slice. The times are simulated.
768 devices in a mesh: dp: 24 (over z, core), group: 32 (over y, x).
Axes of the slice: x: 4, y: 8, z: 12, core: 2. Of those that a mesh axis runs over, the one named last changes fastest.
Arguments:
- embeddings: bfloat16 [98304, 1024], P(('dp', 'group'))
- coarse_lists: int32 [6144, 4], P(('dp', 'group')), may hold values from 0 to 23, all different within a row; in each aligned block of 8 rows (0 to 7, 8 to 15, ...) at most 2 rows name the same one
- home: int32 [32, 24], P('group'), may hold values from 0 to 23, each once within a row
- centroids: bfloat16 [32, 24, 256, 1024], P('group', 'dp')
Outputs:
- new_centroids: float32 [32, 24, 256, 1024], P('group', 'dp')
- weights: float32 [32, 24, 256], P('group', 'dp')
Inputs may be any that keep to these rules, and one draw needn't show every extreme that they name: `coarse_lists`: each row names 4 different block numbers; among the slabs of one device no block number is named more than 2 times. `home`: each row is a permutation.
All inputs are finite; a program needn't handle non-finite values.
Results may differ from a plain program's by a relative error of at most 0.013.
Values may be sent and summed in bfloat16 or wider, within the bound.
No kernel may reach another device: no remote copies, remote signals or barrier semaphores. Data moves between devices by JAX's collectives and lax.ppermute only.
A program may use at most 32 MiB of HBM per device.

v0:
```python
import math

import jax
import jax.numpy as jnp
from jax import lax
from jax.sharding import PartitionSpec as P

ITERS = 2


prior_count = 1.0


def per_device(embeddings, coarse_lists, home, centroids):
    row_count, width = embeddings.shape
    peers = lax.axis_size("dp")
    total_rows = row_count * peers * lax.axis_size("group")
    slab_count, listed_count = coarse_lists.shape
    slab_rows = row_count // slab_count
    most_slabs = max(2, (slab_count * listed_count + peers - 1) // peers)
    capacity = most_slabs * slab_rows
    peer_ids = jnp.arange(peers, dtype=jnp.int32)
    home_row = home[0]
    owner = jnp.sum(jnp.where(coarse_lists[:, :, None] == peer_ids, home_row, 0), axis=2)
    hits = jnp.sum((owner[:, :, None] == peer_ids).astype(jnp.int32), axis=1)
    before = jnp.cumsum(hits, axis=0) - hits
    places = jnp.arange(most_slabs, dtype=jnp.int32)
    matched = hits[:, :, None] * (before[:, :, None] == places).astype(jnp.int32)
    slab_ids = jnp.arange(slab_count, dtype=jnp.int32)
    source_slab = jnp.sum(matched * slab_ids[:, None, None], axis=0)
    filled = jnp.sum(matched, axis=0)
    inner = jnp.arange(slab_rows, dtype=jnp.int32)
    source_row = (source_slab[:, :, None] * slab_rows + inner).reshape(peers, capacity)
    slot_live = jnp.repeat(filled, slab_rows, axis=1).astype(jnp.bfloat16)
    position = jnp.take_along_axis(before, owner, axis=1)
    stat_index = (owner * capacity + position * slab_rows)[:, :, None] + inner[None, None, :]
    squares = lax.psum(jnp.sum(jnp.square(embeddings.astype(jnp.float32)), axis=0), ("dp", "group"))
    feature_scale = lax.rsqrt(squares / total_rows + 1e-06)
    outgoing = (embeddings.astype(jnp.float32) * feature_scale).astype(jnp.bfloat16)
    received, live_slots = (
        lax.all_to_all(outgoing[source_row], "dp", split_axis=0, concat_axis=0, tiled=True),
        lax.all_to_all(slot_live, "dp", split_axis=0, concat_axis=0, tiled=True),
    )
    flat_rows = received.reshape(peers * capacity, width)
    live_flag = live_slots.reshape(-1) > 0
    current = centroids[0, 0].astype(jnp.float32)
    weight_sum = jnp.zeros((current.shape[0],), jnp.float32)
    for turn_index in range(ITERS):
        block_low = current.astype(jnp.bfloat16)
        cnorm = jnp.sum(jnp.square(block_low.astype(jnp.float32)), axis=1)
        products = lax.dot_general(
            flat_rows, block_low, (((1,), (1,)), ((), ())), preferred_element_type=jnp.float32
        )
        logits = (2.0 * products - cnorm[None, :]) / math.sqrt(width)
        largest = jnp.max(logits, axis=1)
        exp_total = jnp.sum(jnp.exp(logits - largest[:, None]), axis=1)
        back_largest, back_total = (
            lax.all_to_all(
                largest.reshape(peers, capacity), "dp", split_axis=0, concat_axis=0, tiled=True
            ),
            lax.all_to_all(
                exp_total.reshape(peers, capacity), "dp", split_axis=0, concat_axis=0, tiled=True
            ),
        )
        their_largest = back_largest.reshape(-1)[stat_index]
        their_total = back_total.reshape(-1)[stat_index]
        summit = jnp.max(their_largest, axis=1)
        row_normal = summit + jnp.log(
            jnp.sum(their_total * jnp.exp(their_largest - summit[:, None, :]), axis=1)
        )
        slot_normal = row_normal.reshape(-1)[source_row]
        owner_normal = lax.all_to_all(
            slot_normal, "dp", split_axis=0, concat_axis=0, tiled=True
        ).reshape(-1)
        resp = jnp.where(live_flag[:, None], jnp.exp(logits - owner_normal[:, None]), 0.0)
        weight_sum = jnp.sum(resp, axis=0)
        sums = lax.dot_general(
            resp.astype(jnp.bfloat16),
            flat_rows,
            (((0,), (0,)), ((), ())),
            preferred_element_type=jnp.float32,
        )
        current = (sums + current) / (weight_sum[:, None] + prior_count)
    return (current[None, None], weight_sum[None, None])


def solution(mesh):
    return jax.shard_map(
        per_device,
        mesh=mesh,
        in_specs=(
            P(("dp", "group"), None),
            P(("dp", "group"), None),
            P("group", None),
            P("group", "dp", None, None),
        ),
        out_specs=(P("group", "dp", None, None), P("group", "dp", None)),
        check_vma=False,
    )
```

profile of v0, /device:TPU:1, one launch (start us, length us, event | category | flops | bytes accessed | tf_op | source)
XLA Modules:
  0.0 308.9 jit_solution(18395683785591795115)
XLA Ops:
  0.7 0.9 select_reduce_fusion
  1.8 1.0 fusion.12
  2.8 120.5 %psum.7 = f32[1024]{0:T(1024)S(1)} all-reduce(f32[1024]{0:T(1024)S(1)} %fusion.12), channel_id=1, replica_groups=mesh['dp'=24,'group'=32] {'dp','group'}, use_global_device_ids=true, to_apply=%region_5.6 | all-reduce | flops 1024 | bytes 8192 | tf_op jit(solution)/shard_map/psum | solution.py:37
  123.5 1.0 fusion.13
  124.5 3.6 %gather_fusion = bf16[768,1024]{1,0:T(8,128)(2,1)} fusion(bf16[128,1024]{1,0:T(8,128)(2,1)S(1)} %fusion.13, s32[1024]{0:T(1024)S(1)} %pad_clamp_fusion.1), kind=kCustom, calls=%fused_computation | custom fusion | bytes 3148800 | tf_op jit(solution)/shard_map/gather | solution.py:41
  128.1 4.7 %all-to-all-start.1 = ((bf16[24,32,1024]{2,1,0:T(8,128)(2,1)}), bf16[24,32,1024]{2,1,0:T(8,128)(2,1)S(1)}, u32[]{:S(2)}, u32[]{:S(2)}) async-start(bf16[24,32,1024]{2,1,0:T(8,128)(2,1)} %bitcast.3), calls=%async_computation.1 | async-start | bytes 3145728 | tf_op jit(solution)/shard_map/all_to_all | solution.py:41
  134.2 54.9 %all-to-all-done.1 = bf16[24,32,1024]{2,1,0:T(8,128)(2,1)S(1)} async-done(((bf16[24,32,1024]{2,1,0:T(8,128)(2,1)}), bf16[24,32,1024]{2,1,0:T(8,128)(2,1)S(1)}, u32[]{:S(2)}, u32[]{:S(2)}) %all-to-all-start.1) | async-done | bytes 1572896 | tf_op jit(solution)/shard_map/all_to_all | solution.py:41
  190.6 5.7 %all-to-all-start.3 = ((f32[24,1,32]{2,1,0:T(1,128)}), f32[24,1,32]{2,1,0:T(1,128)S(1)}, u32[]{:S(2)}, u32[]{:S(2)}) async-start(f32[24,1,32]{2,1,0:T(1,128)} %all_to_all.47), calls=%async_computation.3 | async-start | bytes 24576 | tf_op jit(solution)/shard_map/all_to_all | solution.py:61
  196.4 0.7 all_to_all.45
  197.1 8.5 %all-to-all-done.3 = f32[24,1,32]{2,1,0:T(1,128)S(1)} async-done(((f32[24,1,32]{2,1,0:T(1,128)}), f32[24,1,32]{2,1,0:T(1,128)S(1)}, u32[]{:S(2)}, u32[]{:S(2)}) %all-to-all-start.3) | async-done | bytes 3104 | tf_op jit(solution)/shard_map/all_to_all | solution.py:61
  205.6 4.2 %all-to-all-start.2 = ((f32[24,1,32]{2,1,0:T(1,128)}), f32[24,1,32]{2,1,0:T(1,128)S(1)}, u32[]{:S(2)}, u32[]{:S(2)}) async-start(f32[24,1,32]{2,1,0:T(1,128)} %all_to_all.45), calls=%async_computation.2 | async-start | bytes 24576 | tf_op jit(solution)/shard_map/all_to_all | solution.py:58
  209.8 0.7 copy.27
  211.8 7.5 %all-to-all-done.2 = f32[24,1,32]{2,1,0:T(1,128)S(1)} async-done(((f32[24,1,32]{2,1,0:T(1,128)}), f32[24,1,32]{2,1,0:T(1,128)S(1)}, u32[]{:S(2)}, u32[]{:S(2)}) %all-to-all-start.2) | async-done | bytes 3104 | tf_op jit(solution)/shard_map/all_to_all | solution.py:58
  219.3 4.1 %all-to-all-start = ((bf16[24,1,32]{2,1,0:T(2,128)(2,1)}), bf16[24,1,32]{2,1,0:T(2,128)(2,1)S(1)}, u32[]{:S(2)}, u32[]{:S(2)}) async-start(bf16[24,1,32]{2,1,0:T(2,128)(2,1)} %copy.27), calls=%async_computation | async-start | bytes 24576 | tf_op jit(solution)/shard_map/all_to_all | solution.py:42
  223.4 0.7 reduce.22
  224.2 2.3 gather_fusion.2
  226.5 2.3 gather_fusion.1
  229.1 4.8 %gather_fusion.3 = f32[768]{0:T(1024)S(1)} fusion(f32[128]{0:T(128)S(1)} %add.166, s32[1024]{0:T(1024)S(1)} %pad_clamp_fusion.1), kind=kCustom, calls=%fused_computation.3 | custom fusion | bytes 9216 | tf_op jit(solution)/shard_map/gather | solution.py:71
  233.9 0.7 all_to_all.49
  234.6 9.8 %all-to-all-start.4 = ((f32[24,1,32]{2,1,0:T(1,128)}), f32[24,1,32]{2,1,0:T(1,128)S(1)}, u32[]{:S(2)}, u32[]{:S(2)}) async-start(f32[24,1,32]{2,1,0:T(1,128)} %all_to_all.49), calls=%async_computation.4 | async-start | bytes 24576 | tf_op jit(solution)/shard_map/all_to_all | solution.py:72
  244.5 9.2 %all-to-all-done.4 = f32[24,1,32]{2,1,0:T(1,128)S(1)} async-done(((f32[24,1,32]{2,1,0:T(1,128)}), f32[24,1,32]{2,1,0:T(1,128)S(1)}, u32[]{:S(2)}, u32[]{:S(2)}) %all-to-all-start.4) | async-done | bytes 3104 | tf_op jit(solution)/shard_map/all_to_all | solution.py:72
  254.7 1.8 multiply_reduce_fusion
  257.9 4.2 %all-to-all-start.6 = ((f32[24,1,32]{2,1,0:T(1,128)}), f32[24,1,32]{2,1,0:T(1,128)S(1)}, u32[]{:S(2)}, u32[]{:S(2)}) async-start(f32[24,1,32]{2,1,0:T(1,128)} %all_to_all.53), calls=%async_computation.6 | async-start | bytes 24576 | tf_op jit(solution)/shard_map/all_to_all | solution.py:61
  262.1 0.7 all_to_all.51
  262.8 8.8 %all-to-all-done.6 = f32[24,1,32]{2,1,0:T(1,128)S(1)} async-done(((f32[24,1,32]{2,1,0:T(1,128)}), f32[24,1,32]{2,1,0:T(1,128)S(1)}, u32[]{:S(2)}, u32[]{:S(2)}) %all-to-all-start.6) | async-done | bytes 3104 | tf_op jit(solution)/shard_map/all_to_all | solution.py:61
  271.6 4.1 %all-to-all-start.5 = ((f32[24,1,32]{2,1,0:T(1,128)}), f32[24,1,32]{2,1,0:T(1,128)S(1)}, u32[]{:S(2)}, u32[]{:S(2)}) async-start(f32[24,1,32]{2,1,0:T(1,128)} %all_to_all.51), calls=%async_computation.5 | async-start | bytes 24576 | tf_op jit(solution)/shard_map/all_to_all | solution.py:58
  276.5 2.3 gather_fusion.5
  278.8 6.4 %all-to-all-done.5 = f32[24,1,32]{2,1,0:T(1,128)S(1)} async-done(((f32[24,1,32]{2,1,0:T(1,128)}), f32[24,1,32]{2,1,0:T(1,128)S(1)}, u32[]{:S(2)}, u32[]{:S(2)}) %all-to-all-start.5) | async-done | bytes 3104 | tf_op jit(solution)/shard_map/all_to_all | solution.py:58
  286.0 2.3 gather_fusion.4
  288.6 4.8 %gather_fusion.6 = f32[768]{0:T(1024)S(1)} fusion(f32[128]{0:T(128)S(1)} %add.170, s32[1024]{0:T(1024)S(1)} %pad_clamp_fusion.1), kind=kCustom, calls=%fused_computation.6 | custom fusion | bytes 9216 | tf_op jit(solution)/shard_map/gather | solution.py:71
  293.5 12.8 %all_to_all.65 = f32[24,1,32]{2,1,0:T(1,128)S(1)} all-to-all(f32[24,1,32]{2,1,0:T(1,128)S(1)} %all_to_all.55), channel_id=1, replica_groups=mesh['dp'=24,'group'=32] {'dp'}, dimensions={0} | all-to-all | bytes 6144 | tf_op jit(solution)/shard_map/all_to_all | solution.py:72
  307.3 1.6 fusion.1
  (68 shorter events, 10.6 us)
Async XLA Ops:
  128.1 61.0 %all-to-all-start.1 = ((bf16[24,32,1024]{2,1,0:T(8,128)(2,1)}), bf16[24,32,1024]{2,1,0:T(8,128)(2,1)S(1)}, u32[]{:S(2)}, u32[]{:S(2)}) async-start(bf16[24,32,1024]{2,1,0:T(8,128)(2,1)} %bitcast.3), calls=%async_computation.1 | async-start | bytes 3145728 | tf_op jit(solution)/shard_map/all_to_all | solution.py:41
  133.0 1.0 copy-start
  190.6 15.1 %all-to-all-start.3 = ((f32[24,1,32]{2,1,0:T(1,128)}), f32[24,1,32]{2,1,0:T(1,128)S(1)}, u32[]{:S(2)}, u32[]{:S(2)}) async-start(f32[24,1,32]{2,1,0:T(1,128)} %all_to_all.47), calls=%async_computation.3 | async-start | bytes 24576 | tf_op jit(solution)/shard_map/all_to_all | solution.py:61
  205.6 13.6 %all-to-all-start.2 = ((f32[24,1,32]{2,1,0:T(1,128)}), f32[24,1,32]{2,1,0:T(1,128)S(1)}, u32[]{:S(2)}, u32[]{:S(2)}) async-start(f32[24,1,32]{2,1,0:T(1,128)} %all_to_all.45), calls=%async_computation.2 | async-start | bytes 24576 | tf_op jit(solution)/shard_map/all_to_all | solution.py:58
  219.3 15.3 %all-to-all-start = ((bf16[24,1,32]{2,1,0:T(2,128)(2,1)}), bf16[24,1,32]{2,1,0:T(2,128)(2,1)S(1)}, u32[]{:S(2)}, u32[]{:S(2)}) async-start(bf16[24,1,32]{2,1,0:T(2,128)(2,1)} %copy.27), calls=%async_computation | async-start | bytes 24576 | tf_op jit(solution)/shard_map/all_to_all | solution.py:42
  234.6 19.1 %all-to-all-start.4 = ((f32[24,1,32]{2,1,0:T(1,128)}), f32[24,1,32]{2,1,0:T(1,128)S(1)}, u32[]{:S(2)}, u32[]{:S(2)}) async-start(f32[24,1,32]{2,1,0:T(1,128)} %all_to_all.49), calls=%async_computation.4 | async-start | bytes 24576 | tf_op jit(solution)/shard_map/all_to_all | solution.py:72
  257.9 13.7 %all-to-all-start.6 = ((f32[24,1,32]{2,1,0:T(1,128)}), f32[24,1,32]{2,1,0:T(1,128)S(1)}, u32[]{:S(2)}, u32[]{:S(2)}) async-start(f32[24,1,32]{2,1,0:T(1,128)} %all_to_all.53), calls=%async_computation.6 | async-start | bytes 24576 | tf_op jit(solution)/shard_map/all_to_all | solution.py:61
  271.6 13.6 %all-to-all-start.5 = ((f32[24,1,32]{2,1,0:T(1,128)}), f32[24,1,32]{2,1,0:T(1,128)S(1)}, u32[]{:S(2)}, u32[]{:S(2)}) async-start(f32[24,1,32]{2,1,0:T(1,128)} %all_to_all.51), calls=%async_computation.5 | async-start | bytes 24576 | tf_op jit(solution)/shard_map/all_to_all | solution.py:58
  307.3 1.6 copy-start.1
where the time goes:
time: 310 us; the launch traced here: 309 us
  blocking collectives  133 us (43%)
  waiting for transfers between devices  95.4 us (31%)
  starting transfers between devices  36.7 us (12%)
  local copies, waits for them, and re-layouts  29.5 us (10%)
  other arithmetic  8.39 us (3%)
  matrix products  4.68 us (2%)
    psum x1, blocking collectives, per_device(): lax.psum(jnp.sum(jnp.square(embeddings.astype(jnp.float32)), axis=0), ('d...  120 us
    all_to_all x1, waiting for transfers between devices, per_device(): lax.all_to_all(outgoing[source_row], 'dp', split_axis=0, concat_axis=0, t...  54.9 us
    all_to_all x2, waiting for transfers between devices, per_device(): lax.all_to_all(exp_total.reshape(peers, capacity), 'dp', split_axis=0, co...  17.4 us
    all_to_all x2, waiting for transfers between devices, per_device(): lax.all_to_all(largest.reshape(peers, capacity), 'dp', split_axis=0, conc...  13.9 us
    all_to_all x1, blocking collectives, per_device(): lax.all_to_all(slot_normal, 'dp', split_axis=0, concat_axis=0, tiled=True)  12.8 us
    all_to_all x2, starting transfers between devices, per_device(): lax.all_to_all(exp_total.reshape(peers, capacity), 'dp', split_axis=0, co...  9.84 us
    all_to_all x1, starting transfers between devices, per_device(): lax.all_to_all(slot_normal, 'dp', split_axis=0, concat_axis=0, tiled=True)  9.76 us
    gather x2, local copies, waits for them, and re-layouts, per_device(): slot_normal = row_normal.reshape(-1)[source_row]  9.57 us
  transfers between devices with their start and end apart: 7, of which 6 were waited for; matrix products, arithmetic and copies ran while one was open for 6% of the time, Pallas kernels for 0%

commit v1 on v0

v1 whole, which is shorter than its diff:
```python
import math

import jax
import jax.numpy as jnp
import numpy as np
from jax import lax
from jax.experimental import pallas as pl
from jax.experimental.pallas import tpu as pltpu
from jax.sharding import Mesh, PartitionSpec as P

ITERS = 2
DP = ("z", "core")
LANES = 128

prior_count = 1.0


def vmem(count):
    return [pl.BlockSpec(memory_space=pltpu.VMEM)] * count


def call(body, outs, specs, flops, moved):
    return pl.pallas_call(
        body,
        out_shape=outs,
        in_specs=specs,
        out_specs=tuple(vmem(len(outs))),
        compiler_params=pltpu.CompilerParams(vmem_limit_bytes=40 * 2**20),
        cost_estimate=pl.CostEstimate(flops=flops, bytes_accessed=moved, transcendentals=0),
    )


def dispatch(slab_rows, most, peers, lists_ref, home_ref, emb_ref, out_ref, table):
    slabs, listed = lists_ref.shape

    def clear(p, carry):
        table[p] = 0
        return carry

    lax.fori_loop(0, peers * most, clear, 0)

    def count_clear(p, carry):
        table[peers * most + p] = 0
        return carry

    lax.fori_loop(0, peers, count_clear, 0)

    def place(n, carry):
        slab, k = n // listed, n % listed
        p = home_ref[0, lists_ref[slab, k]]
        seen = table[peers * most + p]
        table[p * most + jnp.minimum(seen, most - 1)] = slab
        table[peers * most + p] = seen + 1
        return carry

    lax.fori_loop(0, slabs * listed, place, 0)

    def copy(n, carry):
        source = pl.multiple_of(table[n] * slab_rows, slab_rows)
        target = pl.multiple_of(n * slab_rows, slab_rows)
        out_ref[pl.ds(target, slab_rows), :] = emb_ref[pl.ds(source, slab_rows), :]
        return carry

    lax.fori_loop(0, peers * most, copy, 0)


def block_stats(block_low, std_ref, logits_ref, stat_ref):
    width = block_low.shape[1]
    peers, rows, lanes = stat_ref.shape
    wide = block_low.astype(jnp.float32)
    cnorm = jnp.sum(wide * wide, axis=1, keepdims=True)
    chunk = 2 * lanes
    lines = []
    for c in range(std_ref.shape[0] // chunk):
        products = lax.dot_general(
            block_low,
            std_ref[c * chunk : (c + 1) * chunk, :],
            (((1,), (1,)), ((), ())),
            preferred_element_type=jnp.float32,
        )
        logits = (2.0 * products - cnorm) * (1.0 / math.sqrt(width))
        logits_ref[:, c * chunk : (c + 1) * chunk] = logits
        largest = jnp.max(logits, axis=0, keepdims=True)
        total = jnp.sum(jnp.exp(logits - largest), axis=0, keepdims=True)
        both = largest + jnp.log(total)
        lines += [both[:, h * lanes : (h + 1) * lanes] for h in range(2)]
    lines += [jnp.zeros((1, lanes), jnp.float32)] * (rows - len(lines))
    stat = jnp.concatenate(lines, axis=0)
    for p in range(peers):
        stat_ref[p] = stat


def first_body(got_ref, scale_ref, block_ref, std_ref, logits_ref, stat_ref):
    chunk = 2 * LANES
    scale = scale_ref[...]
    for c in range(got_ref.shape[0] // chunk):
        at = slice(c * chunk, (c + 1) * chunk)
        std_ref[at, :] = (got_ref[at, :].astype(jnp.float32) * scale).astype(jnp.bfloat16)
    block_stats(block_ref[...], std_ref, logits_ref, stat_ref)


def combine(stats_ref, same_ref, swap_ref, slab_rows):
    peers, rows, lanes = stats_ref.shape
    own = stats_ref[...].reshape(peers * rows, lanes)
    lane = lax.broadcasted_iota(jnp.int32, own.shape, 1)
    ahead = pltpu.roll(own, lanes - slab_rows, 1)
    behind = pltpu.roll(own, slab_rows, 1)
    other = jnp.where(lane % (2 * slab_rows) < slab_rows, ahead, behind)
    own = own.reshape(peers, rows, lanes)
    other = other.reshape(peers, rows, lanes)
    first = jnp.where(same_ref[...] > 0, own, -jnp.inf)
    second = jnp.where(swap_ref[...] > 0, other, -jnp.inf)
    summit = jnp.max(jnp.maximum(first, second), axis=0)
    live = summit > -jnp.inf
    summit = jnp.where(live, summit, 0.0)
    total = jnp.sum(jnp.exp(first - summit) + jnp.exp(second - summit), axis=0)
    return jnp.where(live, summit + jnp.log(jnp.where(live, total, 1.0)), jnp.inf)


def update(normal, logits_ref, std_ref, old):
    lanes = normal.shape[1]
    parts = []
    for r in range(logits_ref.shape[1] // lanes):
        parts.append(jnp.exp(logits_ref[:, r * lanes : (r + 1) * lanes] - normal[r : r + 1, :]))
    resp = jnp.concatenate(parts, axis=1)
    weight = jnp.sum(resp, axis=1, keepdims=True)
    sums = lax.dot_general(
        resp.astype(jnp.bfloat16),
        std_ref[...],
        (((1,), (0,)), ((), ())),
        preferred_element_type=jnp.float32,
    )
    return (sums + old) / (weight + prior_count), weight


def middle_body(
    slab_rows, stats_ref, same_ref, swap_ref, logits_ref, std_ref, old_ref, new_ref, next_ref, stat_ref
):
    normal = combine(stats_ref, same_ref, swap_ref, slab_rows)
    current, _ = update(normal, logits_ref, std_ref, old_ref[...].astype(jnp.float32))
    new_ref[...] = current
    block_stats(current.astype(jnp.bfloat16), std_ref, next_ref, stat_ref)


def last_body(
    slab_rows, stats_ref, same_ref, swap_ref, logits_ref, std_ref, old_ref, new_ref, weight_ref
):
    normal = combine(stats_ref, same_ref, swap_ref, slab_rows)
    current, weight = update(normal, logits_ref, std_ref, old_ref[...].astype(jnp.float32))
    new_ref[...] = current
    flat = jnp.transpose(jnp.broadcast_to(weight, (weight.shape[0], LANES)))
    weight_ref[...] = flat[:1, :]


def spread(x):
    return lax.all_to_all(x, DP, split_axis=0, concat_axis=0, tiled=True)


def per_device(embeddings, coarse_lists, home, centroids):
    row_count, width = embeddings.shape
    peers = lax.axis_size(DP)
    total_rows = row_count * peers * lax.axis_size(("y", "x"))
    slabs, listed = coarse_lists.shape
    slab_rows = row_count // slabs
    most = 2
    slots = peers * most * slab_rows
    f32 = jnp.float32

    with jax.named_scope("sums_and_lists"):
        squares = jnp.sum(jnp.square(embeddings.astype(f32)), axis=0).reshape(-1, LANES)
        names = jnp.pad(coarse_lists.reshape(1, -1).astype(f32), ((0, 0), (0, LANES - slabs * listed)))
        payload = jnp.concatenate([squares, names], axis=0)
        shared = spread(jnp.broadcast_to(payload[None], (peers, *payload.shape)))

    with jax.named_scope("slabs_out"):
        outgoing = pl.pallas_call(
            lambda *refs: dispatch(slab_rows, most, peers, *refs),
            out_shape=jax.ShapeDtypeStruct((slots, width), jnp.bfloat16),
            in_specs=[pl.BlockSpec(memory_space=pltpu.SMEM)] * 2 + vmem(1),
            out_specs=vmem(1)[0],
            scratch_shapes=[pltpu.SMEM((peers * (most + 1),), jnp.int32)],
        )(coarse_lists, home, embeddings)
        received = spread(outgoing.reshape(peers, most * slab_rows, width)).reshape(slots, width)

    with jax.named_scope("feature_scale"):
        total = jnp.sum(shared[:, : width // LANES], axis=0)
        total = lax.psum(lax.psum(total, "x"), "y")
        scale = lax.rsqrt(total / total_rows + 1e-06).reshape(1, width)

    with jax.named_scope("slot_masks"):
        me = lax.axis_index(DP)
        ids = jnp.arange(peers, dtype=jnp.int32)
        lists_all = shared[:, width // LANES, : slabs * listed].astype(jnp.int32)
        home_of = jnp.sum(jnp.where(lists_all[:, :, None] == ids, home[0], 0), axis=2)
        hits = jnp.any(home_of.reshape(peers, slabs, listed)[..., None] == ids, axis=2)
        order = jnp.arange(slabs)
        earlier = (order[None, :] < order[:, None])[None, :, :, None]
        before = jnp.sum(jnp.where(earlier & hits[:, None], 1, 0), axis=2)
        place = jnp.where(hits, before, -1)
        mine = jnp.sum(jnp.where(ids == me, place, 0), axis=2)
        turn = jnp.arange(most)
        chosen = mine[:, None, :] == turn[:, None]

        def lanes_of(wanted):
            found = chosen[..., None] & (place[:, None] == wanted[:, None, None])
            found = jnp.any(found, axis=2).astype(f32)
            found = found.transpose(2, 0, 1).reshape(peers, peers * most)
            found = jnp.repeat(found, slab_rows, axis=1).reshape(peers, -1, LANES)
            return jnp.pad(found, ((0, 0), (0, -found.shape[1] % 8), (0, 0)))

        same, swap = lanes_of(turn), lanes_of(1 - turn)

    block = centroids[0, 0]
    rows_of_stat = same.shape[1]
    work = 2 * slots * block.shape[0] * width
    logits_shape = jax.ShapeDtypeStruct((block.shape[0], slots), f32)
    stat_shape = jax.ShapeDtypeStruct((peers, rows_of_stat, LANES), f32)
    block_shape = jax.ShapeDtypeStruct(block.shape, f32)
    with jax.named_scope("first_logits"):
        std, logits, stat = call(
            first_body,
            (jax.ShapeDtypeStruct((slots, width), jnp.bfloat16), logits_shape, stat_shape),
            vmem(3),
            work,
            4 << 20,
        )(received, scale, block)
    old = block
    for turn_index in range(ITERS - 1):
        with jax.named_scope("stats_out"):
            stats = spread(stat)
        with jax.named_scope("middle_update"):
            old, logits, stat = call(
                lambda *refs: middle_body(slab_rows, *refs),
                (block_shape, logits_shape, stat_shape),
                vmem(6),
                2 * work,
                5 << 20,
            )(stats, same, swap, logits, std, old)
    with jax.named_scope("last_stats_out"):
        stats = spread(stat)
    with jax.named_scope("last_update"):
        current, weight = call(
            lambda *refs: last_body(slab_rows, *refs),
            (block_shape, jax.ShapeDtypeStruct((1, block.shape[0]), f32)),
            vmem(6),
            work,
            5 << 20,
        )(stats, same, swap, logits, std, old)
    return current[None, None], weight[None]


def solution(mesh):
    chips, rows = 12, 8
    grid = np.asarray(mesh.devices).reshape(chips, mesh.devices.shape[0] // chips, rows, -1)
    fine = Mesh(grid, ("z", "core", "y", "x"))
    group = ("y", "x")
    return jax.shard_map(
        per_device,
        mesh=fine,
        in_specs=(P(DP + group, None), P(DP + group, None), P(group, None), P(group, DP, None, None)),
        out_specs=(P(group, DP, None, None), P(group, DP, None)),
        check_vma=False,
    )
```

time: 310 us -> 135 us (0.44)
  blocking collectives: 133 us -> 38.4 us
  waiting for transfers between devices: 95.4 us -> 49.7 us
  local copies, waits for them, and re-layouts: 29.5 us -> 6.41 us
  starting transfers between devices: 36.7 us -> 27.1 us
  Pallas kernels: 0 us -> 8.36 us
  other arithmetic: 8.39 us -> 3.22 us
  matrix products: 4.68 us -> 0 us
    psum x1 -> x2, blocking collectives: 120 us -> 23.7 us  [per_device(): total = lax.psum(lax.psum(total, 'x'), 'y')]
    all_to_all x7 -> x3, waiting for transfers between devices: 95.4 us -> 49.7 us  [spread(): return lax.all_to_all(x, DP, split_axis=0, concat_axis=0, tiled=True)]
    gather x16 -> x0, local copies, waits for them, and re-layouts: 23.6 us -> none  [the longest x2 9.57 us: per_device(): slot_normal = row_normal.reshape(-1)[source_row]]
    all_to_all x7 -> x3, starting transfers between devices: 36.7 us -> 27.1 us  [spread(): return lax.all_to_all(x, DP, split_axis=0, concat_axis=0, tiled=True)]
    pallas_call x0 -> x4, Pallas kernels: none -> 8.36 us  [the longest x1 3.65 us: per_device(): pl.pallas_call(lambda *refs: dispatch(slab_rows, most, peers, *refs), out...]
    dot_general x4 -> x0, matrix products: 4.68 us -> none  [the longest x2 3.37 us: per_device(): lax.dot_general(resp.astype(jnp.bfloat16), flat_rows, (((0,), (0,)), ((),...]
    unnamed x4 -> x11, local copies, waits for them, and re-layouts: 0.11 us -> 4.41 us
    all_to_all x6 -> x0, other arithmetic: 4.07 us -> none  [the longest x2 1.36 us: per_device(): lax.all_to_all(largest.reshape(peers, capacity), 'dp', split_axis=0, conc...]
  transfers between devices with their start and end apart: 7 -> 3, of which waited for: 6 -> 3; matrix products, arithmetic and copies ran while one was open for 6% -> 3% of each run, Pallas kernels for 0% -> 3%
where the time goes in v1:
time: 135 us; the launch traced here: 134 us
  waiting for transfers between devices  49.7 us (37%)
  blocking collectives  38.4 us (28%)
  starting transfers between devices  27.1 us (20%)
  Pallas kernels  8.36 us (6%)
  local copies, waits for them, and re-layouts  6.41 us (5%)
  other arithmetic  3.22 us (2%)
    all_to_all x3, waiting for transfers between devices, spread(): return lax.all_to_all(x, DP, split_axis=0, concat_axis=0, tiled=True)  49.7 us
    all_to_all x3, starting transfers between devices, spread(): return lax.all_to_all(x, DP, split_axis=0, concat_axis=0, tiled=True)  27.1 us
    psum x2, blocking collectives, per_device(): total = lax.psum(lax.psum(total, 'x'), 'y')  23.7 us
    all_to_all x1, blocking collectives, spread(): return lax.all_to_all(x, DP, split_axis=0, concat_axis=0, tiled=True)  14.7 us
    unnamed x11, local copies, waits for them, and re-layouts  4.41 us
    pallas_call x1, Pallas kernels, per_device(): pl.pallas_call(lambda *refs: dispatch(slab_rows, most, peers, *refs), out...  3.65 us
  transfers between devices with their start and end apart: 3, of which 3 were waited for; matrix products, arithmetic and copies ran while one was open for 3% of the time, Pallas kernels for 3%

profile of v1, /device:TPU:1, one launch (start us, length us, event | category | flops | bytes accessed | tf_op | source)
XLA Modules:
  0.0 134.0 jit_solution(10168370459513740066)
XLA Ops:
  0.6 0.7 convert_element_type.43
  1.3 0.1 copy.14
  1.4 0.1 convert_element_type.44
  1.5 1.0 multiply_reduce_fusion
  2.5 0.7 broadcast_in_dim.61
  3.2 16.7 %all-to-all-start.1 = ((f32[24,9,128]{2,1,0:T(8,128)}), f32[24,9,128]{2,1,0:T(8,128)S(1)}, u32[]{:S(2)}, u32[]{:S(2)}) async-start(f32[24,9,128]{2,1,0:T(8,128)} %broadcast_in_dim.61), calls=%async_computation.1 | async-start | bytes 393216 | tf_op jit(solution)/shard_map/sums_and_lists/all_to_all | solution.py:156
  19.9 1.3 %copy.13.refs_0_ = s32[8,4]{1,0:T(8,128)} copy(s32[8,4]{0,1:T(4,128)} %param.5) | data formatting | bytes 256 | tf_op args[1]
  21.3 3.6 %slabs_out.1 = bf16[768,1024]{1,0:T(8,128)(2,1)} custom-call(s32[8,4]{1,0:T(8,128)} %copy.13.refs_0_, s32[1,24]{1,0:T(1,128)} %refs_1_.1, bf16[128,1024]{1,0:T(8,128)(2,1)} %refs_2_.1), custom_call_target="tpu_custom_call" | custom-call | tf_op jit(solution)/shard_map/slabs_out/pallas_call | solution.py:176
  24.9 8.7 %all-to-all-done.1 = f32[24,9,128]{2,1,0:T(8,128)S(1)} async-done(((f32[24,9,128]{2,1,0:T(8,128)}), f32[24,9,128]{2,1,0:T(8,128)S(1)}, u32[]{:S(2)}, u32[]{:S(2)}) %all-to-all-start.1) | async-done | bytes 110624 | tf_op jit(solution)/shard_map/sums_and_lists/all_to_all | solution.py:156
  33.6 4.8 %all-to-all-start = ((bf16[24,32,1024]{2,1,0:T(8,128)(2,1)}), bf16[24,32,1024]{2,1,0:T(8,128)(2,1)S(1)}, u32[]{:S(2)}, u32[]{:S(2)}) async-start(bf16[24,32,1024]{2,1,0:T(8,128)(2,1)} %bitcast.20), calls=%async_computation | async-start | bytes 3145728 | tf_op jit(solution)/shard_map/slabs_out/all_to_all | solution.py:156
  38.5 0.1 select_reduce_fusion.1
  38.8 0.1 copy.16
  38.9 8.9 %psum.14 = f32[8,128]{1,0:T(8,128)S(1)} all-reduce(f32[8,128]{1,0:T(8,128)S(1)} %slice_reduce_fusion), channel_id=1, replica_groups=mesh['z'=12,'core'=2,'y'=8,'x'=4] {'x'}, use_global_device_ids=true, to_apply=%region_2.3 | all-reduce | flops 1024 | bytes 8192 | tf_op jit(solution)/shard_map/feature_scale/psum | solution.py:187
  47.8 14.8 %psum.15 = f32[8,128]{1,0:T(8,128)S(1)} all-reduce(f32[8,128]{1,0:T(8,128)S(1)} %psum.14), channel_id=1, replica_groups=mesh['z'=12,'core'=2,'y'=8,'x'=4] {'y'}, use_global_device_ids=true, to_apply=%region_3.4 | all-reduce | flops 1024 | bytes 8192 | tf_op jit(solution)/shard_map/feature_scale/psum | solution.py:187
  62.6 0.2 fusion
  62.7 0.4 select_reduce_fusion
  63.1 0.5 select_reduce_fusion.2
  63.6 31.3 %all-to-all-done = bf16[24,32,1024]{2,1,0:T(8,128)(2,1)S(1)} async-done(((bf16[24,32,1024]{2,1,0:T(8,128)(2,1)}), bf16[24,32,1024]{2,1,0:T(8,128)(2,1)S(1)}, u32[]{:S(2)}, u32[]{:S(2)}) %all-to-all-start) | async-done | bytes 1572896 | tf_op jit(solution)/shard_map/slabs_out/all_to_all | solution.py:156
  94.9 1.0 copy-done
  96.0 1.5 %first_logits.1 = (bf16[768,1024]{1,0:T(8,128)(2,1)S(1)}, f32[256,768]{1,0:T(8,128)S(1)}, f32[24,8,128]{2,1,0:T(8,128)}) custom-call(bf16[768,1024]{1,0:T(8,128)(2,1)S(1)} %bitcast.16, f32[1,1024]{1,0:T(1,128)S(1)} %bitcast.19, bf16[256,1024]{1,0:T(8,128)(2,1)S(1)} %bitcast.17), custom_call_target="tpu_custom_call" | custom-call | flops 402653184 | bytes 4194304 | tf_op jit(solution)/shard_map/first_logits/pallas_call | solution.py:220
  97.5 0.9 copy-done.2
  98.4 5.6 %all-to-all-start.2 = ((f32[24,8,128]{2,1,0:T(8,128)}), f32[24,8,128]{2,1,0:T(8,128)S(1)}, u32[]{:S(2)}, u32[]{:S(2)}) async-start(f32[24,8,128]{2,1,0:T(8,128)} %get-tuple-element.10), calls=%async_computation.2 | async-start | bytes 196608 | tf_op jit(solution)/shard_map/stats_out/all_to_all | solution.py:156
  104.0 0.3 and_reduce_fusion
  104.4 0.2 broadcast_in_dim.69
  104.7 0.2 reshape.90
  104.9 0.2 broadcast_in_dim.70
  105.1 0.2 reshape.93
  105.3 9.7 %all-to-all-done.2.refs_0_ = f32[24,8,128]{2,1,0:T(8,128)S(1)} async-done(((f32[24,8,128]{2,1,0:T(8,128)}), f32[24,8,128]{2,1,0:T(8,128)S(1)}, u32[]{:S(2)}, u32[]{:S(2)}) %all-to-all-start.2) | async-done | bytes 98336 | tf_op jit(solution)/shard_map/stats_out/all_to_all | solution.py:156
  115.0 1.1 copy-done.3
  116.2 1.4 %middle_update.1 = (f32[256,1024]{1,0:T(8,128)S(1)}, f32[256,768]{1,0:T(8,128)S(1)}, f32[24,8,128]{2,1,0:T(8,128)S(1)}) custom-call(f32[24,8,128]{2,1,0:T(8,128)S(1)} %all-to-all-done.2.refs_0_, f32[24,8,128]{2,1,0:T(8,128)S(1)} %pad.12.refs_1_, f32[24,8,128]{2,1,0:T(8,128)S(1)} %pad.13.refs_2_, f32[256,768]{1,0:T(8,128)S(1)} %copy-done.3, ...), custom_call_target="tpu_custom_call" | custom-call | flops 805306368 | bytes 5242880 | tf_op jit(solution)/shard_map/middle_update/pallas_call | solution.py:232
  117.6 14.7 %all_to_all.20.refs_0_ = f32[24,8,128]{2,1,0:T(8,128)S(1)} all-to-all(f32[24,8,128]{2,1,0:T(8,128)S(1)} %get-tuple-element.13), channel_id=1, replica_groups=mesh['z'=12,'core'=2,'y'=8,'x'=4] {'z','core'}, dimensions={0} | all-to-all | bytes 196608 | tf_op jit(solution)/shard_map/last_stats_out/all_to_all | solution.py:156
  132.3 1.8 %last_update.1 = (f32[256,1024]{1,0:T(8,128)}, f32[1,256]{1,0:T(1,128)}) custom-call(f32[24,8,128]{2,1,0:T(8,128)S(1)} %all_to_all.20.refs_0_, f32[24,8,128]{2,1,0:T(8,128)S(1)} %pad.12.refs_1_, f32[24,8,128]{2,1,0:T(8,128)S(1)} %pad.13.refs_2_, f32[256,768]{1,0:T(8,128)S(1)} %get-tuple-element.14.refs_3_, bf16[768,1024]{1,0:T(8,128)(2,1)S(1)} %get-tuple-element.12.refs_4_, ...), custom_call_target="tpu_custom_call" | custom-call | flops 402653184 | bytes 5242880 | tf_op jit(solution)/shard_map/last_update/pallas_call | solution.py:242
  (22 shorter events, 0.4 us)
Async XLA Ops:
  3.2 30.4 %all-to-all-start.1 = ((f32[24,9,128]{2,1,0:T(8,128)}), f32[24,9,128]{2,1,0:T(8,128)S(1)}, u32[]{:S(2)}, u32[]{:S(2)}) async-start(f32[24,9,128]{2,1,0:T(8,128)} %broadcast_in_dim.61), calls=%async_computation.1 | async-start | bytes 393216 | tf_op jit(solution)/shard_map/sums_and_lists/all_to_all | solution.py:156
  33.6 4.9 %copy-start.4 = (s32[1,24]{1,0:T(1,128)S(1)}, s32[1,24]{1,0:T(1,128)}, u32[]{:S(2)}) copy-start(s32[1,24]{1,0:T(1,128)} %refs_1_.1) | copy-start | bytes 292
  33.6 61.3 %all-to-all-start = ((bf16[24,32,1024]{2,1,0:T(8,128)(2,1)}), bf16[24,32,1024]{2,1,0:T(8,128)(2,1)S(1)}, u32[]{:S(2)}, u32[]{:S(2)}) async-start(bf16[24,32,1024]{2,1,0:T(8,128)(2,1)} %bitcast.20), calls=%async_computation | async-start | bytes 3145728 | tf_op jit(solution)/shard_map/slabs_out/all_to_all | solution.py:156
  94.9 1.0 copy-start
  97.5 0.9 copy-start.2
  98.4 16.7 %all-to-all-start.2 = ((f32[24,8,128]{2,1,0:T(8,128)}), f32[24,8,128]{2,1,0:T(8,128)S(1)}, u32[]{:S(2)}, u32[]{:S(2)}) async-start(f32[24,8,128]{2,1,0:T(8,128)} %get-tuple-element.10), calls=%async_computation.2 | async-start | bytes 196608 | tf_op jit(solution)/shard_map/stats_out/all_to_all | solution.py:156
  104.2 10.8 %copy-start.1 = (bf16[1,1,256,1024]{3,2,1,0:T(8,128)(2,1)S(1)}, bf16[1,1,256,1024]{3,2,1,0:T(8,128)(2,1)}, u32[]{:S(2)}) copy-start(bf16[1,1,256,1024]{3,2,1,0:T(8,128)(2,1)} %param.7) | copy-start | bytes 1572868
  115.0 1.1 copy-start.3

commit v2 on v1

--- a/solution.py
+++ b/solution.py
@@ -25,13 +25,27 @@
         out_shape=outs,
         in_specs=specs,
         out_specs=tuple(vmem(len(outs))),
-        compiler_params=pltpu.CompilerParams(vmem_limit_bytes=40 * 2**20),
+        compiler_params=pltpu.CompilerParams(vmem_limit_bytes=16 * 2**20),
         cost_estimate=pl.CostEstimate(flops=flops, bytes_accessed=moved, transcendentals=0),
     )
 
 
+def share_body(lists_ref, emb_ref, out_ref):
+    listed, slabs = lists_ref.shape
+    wide = emb_ref[...].astype(jnp.float32)
+    squares = jnp.sum(wide * wide, axis=0, keepdims=True)
+    lines = [squares[:, c : c + LANES] for c in range(0, wide.shape[1], LANES)]
+    lane = lax.broadcasted_iota(jnp.int32, (1, LANES), 1)
+    names = jnp.zeros((1, LANES), jnp.int32)
+    for n in range(slabs * listed):
+        names = jnp.where(lane == n, lists_ref[n % listed, n // listed], names)
+    payload = jnp.concatenate([*lines, names.astype(jnp.float32)], axis=0)
+    for p in range(out_ref.shape[0]):
+        out_ref[p] = payload
+
+
 def dispatch(slab_rows, most, peers, lists_ref, home_ref, emb_ref, out_ref, table):
-    slabs, listed = lists_ref.shape
+    listed, slabs = lists_ref.shape
 
     def clear(p, carry):
         table[p] = 0
@@ -47,7 +61,7 @@
 
     def place(n, carry):
         slab, k = n // listed, n % listed
-        p = home_ref[0, lists_ref[slab, k]]
+        p = home_ref[0, lists_ref[k, slab]]
         seen = table[peers * most + p]
         table[p * most + jnp.minimum(seen, most - 1)] = slab
         table[peers * most + p] = seen + 1
@@ -64,22 +78,27 @@
     lax.fori_loop(0, peers * most, copy, 0)
 
 
-def block_stats(block_low, std_ref, logits_ref, stat_ref):
+def block_logits(block_low, std_ref):
     width = block_low.shape[1]
-    peers, rows, lanes = stat_ref.shape
     wide = block_low.astype(jnp.float32)
     cnorm = jnp.sum(wide * wide, axis=1, keepdims=True)
-    chunk = 2 * lanes
-    lines = []
-    for c in range(std_ref.shape[0] // chunk):
+    chunk = 2 * LANES
+    for c in range(0, std_ref.shape[0], chunk):
         products = lax.dot_general(
             block_low,
-            std_ref[c * chunk : (c + 1) * chunk, :],
+            std_ref[c : c + chunk, :],
             (((1,), (1,)), ((), ())),
             preferred_element_type=jnp.float32,
         )
-        logits = (2.0 * products - cnorm) * (1.0 / math.sqrt(width))
-        logits_ref[:, c * chunk : (c + 1) * chunk] = logits
+        yield c, chunk, (2.0 * products - cnorm) * (1.0 / math.sqrt(width))
+
+
+def block_stats(block_low, std_ref, stat_ref, logits_ref=None):
+    peers, rows, lanes = stat_ref.shape
+    lines = []
+    for c, chunk, logits in block_logits(block_low, std_ref):
+        if logits_ref is not None:
+            logits_ref[:, c : c + chunk] = logits
         largest = jnp.max(logits, axis=0, keepdims=True)
         total = jnp.sum(jnp.exp(logits - largest), axis=0, keepdims=True)
         both = largest + jnp.log(total)
@@ -90,13 +109,13 @@
         stat_ref[p] = stat
 
 
-def first_body(got_ref, scale_ref, block_ref, std_ref, logits_ref, stat_ref):
+def first_body(got_ref, scale_ref, block_ref, std_ref, stat_ref):
     chunk = 2 * LANES
-    scale = scale_ref[...]
+    scale = jnp.concatenate([scale_ref[r : r + 1, :] for r in range(scale_ref.shape[0])], axis=1)
     for c in range(got_ref.shape[0] // chunk):
         at = slice(c * chunk, (c + 1) * chunk)
         std_ref[at, :] = (got_ref[at, :].astype(jnp.float32) * scale).astype(jnp.bfloat16)
-    block_stats(block_ref[...], std_ref, logits_ref, stat_ref)
+    block_stats(block_ref[...], std_ref, stat_ref)
 
 
 def combine(stats_ref, same_ref, swap_ref, slab_rows):
@@ -117,11 +136,12 @@
     return jnp.where(live, summit + jnp.log(jnp.where(live, total, 1.0)), jnp.inf)
 
 
-def update(normal, logits_ref, std_ref, old):
-    lanes = normal.shape[1]
+def update(normal, logits, std_ref, old):
     parts = []
-    for r in range(logits_ref.shape[1] // lanes):
-        parts.append(jnp.exp(logits_ref[:, r * lanes : (r + 1) * lanes] - normal[r : r + 1, :]))
+    for c, chunk, values in logits:
+        for h in range(0, chunk, LANES):
+            r = (c + h) // LANES
+            parts.append(jnp.exp(values[:, h : h + LANES] - normal[r : r + 1, :]))
     resp = jnp.concatenate(parts, axis=1)
     weight = jnp.sum(resp, axis=1, keepdims=True)
     sums = lax.dot_general(
@@ -134,19 +154,30 @@
 
 
 def middle_body(
-    slab_rows, stats_ref, same_ref, swap_ref, logits_ref, std_ref, old_ref, new_ref, next_ref, stat_ref
+    slab_rows,
+    stats_ref,
+    same_ref,
+    swap_ref,
+    std_ref,
+    old_ref,
+    new_ref,
+    next_ref,
+    stat_ref,
 ):
     normal = combine(stats_ref, same_ref, swap_ref, slab_rows)
-    current, _ = update(normal, logits_ref, std_ref, old_ref[...].astype(jnp.float32))
+    old = old_ref[...]
+    logits = block_logits(old.astype(jnp.bfloat16), std_ref)
+    current, _ = update(normal, logits, std_ref, old.astype(jnp.float32))
     new_ref[...] = current
-    block_stats(current.astype(jnp.bfloat16), std_ref, next_ref, stat_ref)
+    block_stats(current.astype(jnp.bfloat16), std_ref, stat_ref, next_ref)
 
 
 def last_body(
     slab_rows, stats_ref, same_ref, swap_ref, logits_ref, std_ref, old_ref, new_ref, weight_ref
 ):
     normal = combine(stats_ref, same_ref, swap_ref, slab_rows)
-    current, weight = update(normal, logits_ref, std_ref, old_ref[...].astype(jnp.float32))
+    logits = [(0, logits_ref.shape[1], logits_ref[...])]
+    current, weight = update(normal, logits, std_ref, old_ref[...])
     new_ref[...] = current
     flat = jnp.transpose(jnp.broadcast_to(weight, (weight.shape[0], LANES)))
     weight_ref[...] = flat[:1, :]
@@ -167,10 +198,14 @@
     f32 = jnp.float32
 
     with jax.named_scope("sums_and_lists"):
-        squares = jnp.sum(jnp.square(embeddings.astype(f32)), axis=0).reshape(-1, LANES)
-        names = jnp.pad(coarse_lists.reshape(1, -1).astype(f32), ((0, 0), (0, LANES - slabs * listed)))
-        payload = jnp.concatenate([squares, names], axis=0)
-        shared = spread(jnp.broadcast_to(payload[None], (peers, *payload.shape)))
+        lists = coarse_lists.T
+        payload = pl.pallas_call(
+            share_body,
+            out_shape=jax.ShapeDtypeStruct((peers, width // LANES + 1, LANES), f32),
+            in_specs=[pl.BlockSpec(memory_space=pltpu.SMEM)] + vmem(1),
+            out_specs=vmem(1)[0],
+        )(lists, embeddings)
+        shared = spread(payload)
 
     with jax.named_scope("slabs_out"):
         outgoing = pl.pallas_call(
@@ -179,13 +214,13 @@
             in_specs=[pl.BlockSpec(memory_space=pltpu.SMEM)] * 2 + vmem(1),
             out_specs=vmem(1)[0],
             scratch_shapes=[pltpu.SMEM((peers * (most + 1),), jnp.int32)],
-        )(coarse_lists, home, embeddings)
+        )(lists, home, embeddings)
         received = spread(outgoing.reshape(peers, most * slab_rows, width)).reshape(slots, width)
 
     with jax.named_scope("feature_scale"):
         total = jnp.sum(shared[:, : width // LANES], axis=0)
         total = lax.psum(lax.psum(total, "x"), "y")
-        scale = lax.rsqrt(total / total_rows + 1e-06).reshape(1, width)
+        scale = lax.rsqrt(total / total_rows + 1e-06)
 
     with jax.named_scope("slot_masks"):
         me = lax.axis_index(DP)
@@ -217,9 +252,9 @@
     stat_shape = jax.ShapeDtypeStruct((peers, rows_of_stat, LANES), f32)
     block_shape = jax.ShapeDtypeStruct(block.shape, f32)
     with jax.named_scope("first_logits"):
-        std, logits, stat = call(
+        std, stat = call(
             first_body,
-            (jax.ShapeDtypeStruct((slots, width), jnp.bfloat16), logits_shape, stat_shape),
+            (jax.ShapeDtypeStruct((slots, width), jnp.bfloat16), stat_shape),
             vmem(3),
             work,
             4 << 20,
@@ -232,10 +267,10 @@
             old, logits, stat = call(
                 lambda *refs: middle_body(slab_rows, *refs),
                 (block_shape, logits_shape, stat_shape),
-                vmem(6),
-                2 * work,
+                vmem(5),
+                3 * work,
                 5 << 20,
-            )(stats, same, swap, logits, std, old)
+            )(stats, same, swap, std, old)
     with jax.named_scope("last_stats_out"):
         stats = spread(stat)
     with jax.named_scope("last_update"):

time: 135 us -> 132 us (0.978)
  local copies, waits for them, and re-layouts: 6.41 us -> 2.2 us
  Pallas kernels: 8.36 us -> 10.5 us
  other arithmetic: 3.22 us -> 1.5 us
    unnamed x11 -> x6, local copies, waits for them, and re-layouts: 4.41 us -> 1.05 us
    pallas_call x1 -> x2, Pallas kernels: 1.53 us -> 3.26 us  [the longest x1 1.68 us: per_device(): pl.pallas_call(share_body, out_shape=jax.ShapeDtypeStruct((peers, width /...]
  transfers between devices with their start and end apart: 3 -> 3, of which waited for: 3 -> 3; matrix products, arithmetic and copies ran while one was open for 3% -> 2% of each run, Pallas kernels for 3% -> 3%
where the time goes in v2:
time: 132 us; the launch traced here: 131 us
  waiting for transfers between devices  51 us (39%)
  blocking collectives  38.4 us (29%)
  starting transfers between devices  27.1 us (21%)
  Pallas kernels  10.5 us (8%)
  local copies, waits for them, and re-layouts  2.2 us (2%)
  other arithmetic  1.5 us (1%)
    all_to_all x3, waiting for transfers between devices, spread(): return lax.all_to_all(x, DP, split_axis=0, concat_axis=0, tiled=True)  51 us
    all_to_all x3, starting transfers between devices, spread(): return lax.all_to_all(x, DP, split_axis=0, concat_axis=0, tiled=True)  27.1 us
    psum x2, blocking collectives, per_device(): total = lax.psum(lax.psum(total, 'x'), 'y')  23.7 us
    all_to_all x1, blocking collectives, spread(): return lax.all_to_all(x, DP, split_axis=0, concat_axis=0, tiled=True)  14.7 us
    pallas_call x1, Pallas kernels, per_device(): pl.pallas_call(lambda *refs: dispatch(slab_rows, most, peers, *refs), out...  3.67 us
  transfers between devices with their start and end apart: 3, of which 3 were waited for; matrix products, arithmetic and copies ran while one was open for 2% of the time, Pallas kernels for 3%

profile of v2, /device:TPU:1, one launch (start us, length us, event | category | flops | bytes accessed | tf_op | source)
XLA Modules:
  0.0 131.5 jit_solution(17680291664871341277)
XLA Ops:
  0.6 1.7 %sums_and_lists.1 = f32[24,9,128]{2,1,0:T(8,128)} custom-call(s32[4,8]{1,0:T(4,128)} %bitcast.23, bf16[128,1024]{1,0:T(8,128)(2,1)} %emb_ref.1), custom_call_target="tpu_custom_call" | custom-call | tf_op jit(solution)/shard_map/sums_and_lists/pallas_call | solution.py:202
  2.3 16.7 %all-to-all-start.1 = ((f32[24,9,128]{2,1,0:T(8,128)}), f32[24,9,128]{2,1,0:T(8,128)S(1)}, u32[]{:S(2)}, u32[]{:S(2)}) async-start(f32[24,9,128]{2,1,0:T(8,128)} %sums_and_lists.1), calls=%async_computation.1 | async-start | bytes 393216 | tf_op jit(solution)/shard_map/sums_and_lists/all_to_all | solution.py:187
  19.0 3.7 %slabs_out.1 = bf16[768,1024]{1,0:T(8,128)(2,1)} custom-call(s32[4,8]{1,0:T(4,128)} %bitcast.24, s32[1,24]{1,0:T(1,128)} %refs_1_.1, bf16[128,1024]{1,0:T(8,128)(2,1)} %emb_ref.1), custom_call_target="tpu_custom_call" | custom-call | tf_op jit(solution)/shard_map/slabs_out/pallas_call | solution.py:211
  22.7 10.1 %all-to-all-done.1 = f32[24,9,128]{2,1,0:T(8,128)S(1)} async-done(((f32[24,9,128]{2,1,0:T(8,128)}), f32[24,9,128]{2,1,0:T(8,128)S(1)}, u32[]{:S(2)}, u32[]{:S(2)}) %all-to-all-start.1) | async-done | bytes 110624 | tf_op jit(solution)/shard_map/sums_and_lists/all_to_all | solution.py:187
  32.7 0.0 copy-start.2
  32.7 4.8 %all-to-all-start = ((bf16[24,32,1024]{2,1,0:T(8,128)(2,1)}), bf16[24,32,1024]{2,1,0:T(8,128)(2,1)S(1)}, u32[]{:S(2)}, u32[]{:S(2)}) async-start(bf16[24,32,1024]{2,1,0:T(8,128)(2,1)} %bitcast.18), calls=%async_computation | async-start | bytes 3145728 | tf_op jit(solution)/shard_map/slabs_out/all_to_all | solution.py:187
  37.6 0.0 copy-done.2
  37.7 0.1 select_reduce_fusion.1
  37.8 0.1 copy.9
  37.9 0.1 copy.10
  38.0 8.9 %psum.14 = f32[8,128]{1,0:T(8,128)S(1)} all-reduce(f32[8,128]{1,0:T(8,128)S(1)} %slice_reduce_fusion), channel_id=1, replica_groups=mesh['z'=12,'core'=2,'y'=8,'x'=4] {'x'}, use_global_device_ids=true, to_apply=%region_1.0 | all-reduce | flops 1024 | bytes 8192 | tf_op jit(solution)/shard_map/feature_scale/psum | solution.py:222
  46.9 14.8 %psum.15 = f32[8,128]{1,0:T(8,128)S(1)} all-reduce(f32[8,128]{1,0:T(8,128)S(1)} %psum.14), channel_id=1, replica_groups=mesh['z'=12,'core'=2,'y'=8,'x'=4] {'y'}, use_global_device_ids=true, to_apply=%region_2.0 | all-reduce | flops 1024 | bytes 8192 | tf_op jit(solution)/shard_map/feature_scale/psum | solution.py:222
  61.7 0.2 fusion
  61.8 0.4 select_reduce_fusion
  62.2 0.5 select_reduce_fusion.2
  62.7 31.3 %all-to-all-done = bf16[24,32,1024]{2,1,0:T(8,128)(2,1)S(1)} async-done(((bf16[24,32,1024]{2,1,0:T(8,128)(2,1)}), bf16[24,32,1024]{2,1,0:T(8,128)(2,1)S(1)}, u32[]{:S(2)}, u32[]{:S(2)}) %all-to-all-start) | async-done | bytes 1572896 | tf_op jit(solution)/shard_map/slabs_out/all_to_all | solution.py:187
  94.0 1.0 copy-done
  95.1 1.6 %first_logits.1 = (bf16[768,1024]{1,0:T(8,128)(2,1)S(1)}, f32[24,8,128]{2,1,0:T(8,128)}) custom-call(bf16[768,1024]{1,0:T(8,128)(2,1)S(1)} %bitcast.15, f32[8,128]{1,0:T(8,128)S(1)} %add_rsqrt_fusion.scale_ref, bf16[256,1024]{1,0:T(8,128)(2,1)S(1)} %bitcast.16), custom_call_target="tpu_custom_call" | custom-call | flops 402653184 | bytes 4194304 | tf_op jit(solution)/shard_map/first_logits/pallas_call | solution.py:255
  96.6 5.6 %all-to-all-start.2 = ((f32[24,8,128]{2,1,0:T(8,128)}), f32[24,8,128]{2,1,0:T(8,128)S(1)}, u32[]{:S(2)}, u32[]{:S(2)}) async-start(f32[24,8,128]{2,1,0:T(8,128)} %get-tuple-element.9), calls=%async_computation.2 | async-start | bytes 196608 | tf_op jit(solution)/shard_map/stats_out/all_to_all | solution.py:187
  102.3 0.3 and_reduce_fusion
  102.5 0.0 copy-start.1
  102.5 0.1 copy.12
  102.6 0.1 copy.11
  102.7 0.2 broadcast_in_dim.62
  102.9 0.2 reshape.67
  103.1 0.2 broadcast_in_dim.63
  103.4 0.2 reshape.70
  103.6 9.7 %all-to-all-done.2.refs_0_ = f32[24,8,128]{2,1,0:T(8,128)S(1)} async-done(((f32[24,8,128]{2,1,0:T(8,128)}), f32[24,8,128]{2,1,0:T(8,128)S(1)}, u32[]{:S(2)}, u32[]{:S(2)}) %all-to-all-start.2) | async-done | bytes 98336 | tf_op jit(solution)/shard_map/stats_out/all_to_all | solution.py:187
  113.3 0.0 copy-done.1
  113.3 1.8 %middle_update.1 = (f32[256,1024]{1,0:T(8,128)S(1)}, f32[256,768]{1,0:T(8,128)S(1)}, f32[24,8,128]{2,1,0:T(8,128)S(1)}) custom-call(f32[24,8,128]{2,1,0:T(8,128)S(1)} %all-to-all-done.2.refs_0_, f32[24,8,128]{2,1,0:T(8,128)S(1)} %pad.7.refs_1_, f32[24,8,128]{2,1,0:T(8,128)S(1)} %pad.8.refs_2_, bf16[768,1024]{1,0:T(8,128)(2,1)S(1)} %get-tuple-element.10.refs_3_.refs_4_, ...), custom_call_target="tpu_custom_call" | custom-call | flops 1207959552 | bytes 5242880 | tf_op jit(solution)/shard_map/middle_update/pallas_call | solution.py:267
  115.1 14.7 %all_to_all.20.refs_0_ = f32[24,8,128]{2,1,0:T(8,128)S(1)} all-to-all(f32[24,8,128]{2,1,0:T(8,128)S(1)} %get-tuple-element.11), channel_id=1, replica_groups=mesh['z'=12,'core'=2,'y'=8,'x'=4] {'z','core'}, dimensions={0} | all-to-all | bytes 196608 | tf_op jit(solution)/shard_map/last_stats_out/all_to_all | solution.py:187
  129.7 1.8 %last_update.1 = (f32[256,1024]{1,0:T(8,128)}, f32[1,256]{1,0:T(1,128)}) custom-call(f32[24,8,128]{2,1,0:T(8,128)S(1)} %all_to_all.20.refs_0_, f32[24,8,128]{2,1,0:T(8,128)S(1)} %pad.7.refs_1_, f32[24,8,128]{2,1,0:T(8,128)S(1)} %pad.8.refs_2_, f32[256,768]{1,0:T(8,128)S(1)} %get-tuple-element.12.refs_3_, ...), custom_call_target="tpu_custom_call" | custom-call | flops 402653184 | bytes 5242880 | tf_op jit(solution)/shard_map/last_update/pallas_call | solution.py:277
  (12 shorter events, 0.1 us)
Async XLA Ops:
  2.3 30.4 %all-to-all-start.1 = ((f32[24,9,128]{2,1,0:T(8,128)}), f32[24,9,128]{2,1,0:T(8,128)S(1)}, u32[]{:S(2)}, u32[]{:S(2)}) async-start(f32[24,9,128]{2,1,0:T(8,128)} %sums_and_lists.1), calls=%async_computation.1 | async-start | bytes 393216 | tf_op jit(solution)/shard_map/sums_and_lists/all_to_all | solution.py:187
  32.7 4.9 %copy-start.2 = (s32[1,24]{1,0:T(1,128)S(1)}, s32[1,24]{1,0:T(1,128)}, u32[]{:S(2)}) copy-start(s32[1,24]{1,0:T(1,128)} %refs_1_.1) | copy-start | bytes 292
  32.7 61.3 %all-to-all-start = ((bf16[24,32,1024]{2,1,0:T(8,128)(2,1)}), bf16[24,32,1024]{2,1,0:T(8,128)(2,1)S(1)}, u32[]{:S(2)}, u32[]{:S(2)}) async-start(bf16[24,32,1024]{2,1,0:T(8,128)(2,1)} %bitcast.18), calls=%async_computation | async-start | bytes 3145728 | tf_op jit(solution)/shard_map/slabs_out/all_to_all | solution.py:187
  94.0 1.0 copy-start
  96.6 16.6 %all-to-all-start.2 = ((f32[24,8,128]{2,1,0:T(8,128)}), f32[24,8,128]{2,1,0:T(8,128)S(1)}, u32[]{:S(2)}, u32[]{:S(2)}) async-start(f32[24,8,128]{2,1,0:T(8,128)} %get-tuple-element.9), calls=%async_computation.2 | async-start | bytes 196608 | tf_op jit(solution)/shard_map/stats_out/all_to_all | solution.py:187
  102.5 10.8 %copy-start.1 = (bf16[1,1,256,1024]{3,2,1,0:T(8,128)(2,1)S(1)}, bf16[1,1,256,1024]{3,2,1,0:T(8,128)(2,1)}, u32[]{:S(2)}) copy-start(bf16[1,1,256,1024]{3,2,1,0:T(8,128)(2,1)} %param.7) | copy-start | bytes 1572868

commit v3 on v2

--- a/solution.py
+++ b/solution.py
@@ -109,7 +109,7 @@
         stat_ref[p] = stat
 
 
-def first_body(got_ref, scale_ref, block_ref, std_ref, stat_ref):
+def first_body(got_ref, scale_ref, block_ref, same_ref, swap_ref, std_ref, stat_ref):
     chunk = 2 * LANES
     scale = jnp.concatenate([scale_ref[r : r + 1, :] for r in range(scale_ref.shape[0])], axis=1)
     for c in range(got_ref.shape[0] // chunk):
@@ -255,10 +255,10 @@
         std, stat = call(
             first_body,
             (jax.ShapeDtypeStruct((slots, width), jnp.bfloat16), stat_shape),
-            vmem(3),
+            vmem(5),
             work,
             4 << 20,
-        )(received, scale, block)
+        )(received, scale, block, same, swap)
     old = block
     for turn_index in range(ITERS - 1):
         with jax.named_scope("stats_out"):

time: 132 us -> 130 us (0.985)
  blocking collectives: 38.4 us -> 55.2 us
  waiting for transfers between devices: 51 us -> 39.6 us
  starting transfers between devices: 27.1 us -> 21.5 us
    all_to_all x1 -> x2, blocking collectives: 14.7 us -> 31.1 us  [spread(): return lax.all_to_all(x, DP, split_axis=0, concat_axis=0, tiled=True)]
    all_to_all x3 -> x2, waiting for transfers between devices: 51 us -> 39.6 us  [spread(): return lax.all_to_all(x, DP, split_axis=0, concat_axis=0, tiled=True)]
    all_to_all x3 -> x2, starting transfers between devices: 27.1 us -> 21.5 us  [spread(): return lax.all_to_all(x, DP, split_axis=0, concat_axis=0, tiled=True)]
  transfers between devices with their start and end apart: 3 -> 2, of which waited for: 3 -> 2; matrix products, arithmetic and copies ran while one was open for 2% -> 2% of each run, Pallas kernels for 3% -> 3%
where the time goes in v3:
time: 130 us
  blocking collectives  55.2 us (42%)
  waiting for transfers between devices  39.6 us (30%)
  starting transfers between devices  21.5 us (17%)
  Pallas kernels  9.81 us (8%)
  other arithmetic  1.52 us (1%)
    all_to_all x2, waiting for transfers between devices, spread(): return lax.all_to_all(x, DP, split_axis=0, concat_axis=0, tiled=True)  39.6 us
    all_to_all x2, blocking collectives, spread(): return lax.all_to_all(x, DP, split_axis=0, concat_axis=0, tiled=True)  31.1 us
    psum x2, blocking collectives, per_device(): total = lax.psum(lax.psum(total, 'x'), 'y')  24.1 us
    all_to_all x2, starting transfers between devices, spread(): return lax.all_to_all(x, DP, split_axis=0, concat_axis=0, tiled=True)  21.5 us
    pallas_call x1, Pallas kernels, per_device(): pl.pallas_call(lambda *refs: dispatch(slab_rows, most, peers, *refs), out...  3.67 us
  transfers between devices with their start and end apart: 2, of which 2 were waited for; matrix products, arithmetic and copies ran while one was open for 2% of the time, Pallas kernels for 3%

profile of v3, /device:TPU:1, one launch (start us, length us, event | category | flops | bytes accessed | tf_op | source)
XLA Modules:
  0.0 129.6 jit_solution(10048150896264433192)
XLA Ops:
  0.6 1.7 %sums_and_lists.1 = f32[24,9,128]{2,1,0:T(8,128)} custom-call(s32[4,8]{1,0:T(4,128)} %bitcast.23, bf16[128,1024]{1,0:T(8,128)(2,1)} %emb_ref.1), custom_call_target="tpu_custom_call" | custom-call | tf_op jit(solution)/shard_map/sums_and_lists/pallas_call | solution.py:202
  2.3 16.7 %all-to-all-start.1 = ((f32[24,9,128]{2,1,0:T(8,128)}), f32[24,9,128]{2,1,0:T(8,128)S(1)}, u32[]{:S(2)}, u32[]{:S(2)}) async-start(f32[24,9,128]{2,1,0:T(8,128)} %sums_and_lists.1), calls=%async_computation.1 | async-start | bytes 393216 | tf_op jit(solution)/shard_map/sums_and_lists/all_to_all | solution.py:187
  19.0 3.7 %slabs_out.1 = bf16[768,1024]{1,0:T(8,128)(2,1)} custom-call(s32[4,8]{1,0:T(4,128)} %bitcast.24, s32[1,24]{1,0:T(1,128)} %refs_1_.1, bf16[128,1024]{1,0:T(8,128)(2,1)} %emb_ref.1), custom_call_target="tpu_custom_call" | custom-call | tf_op jit(solution)/shard_map/slabs_out/pallas_call | solution.py:211
  22.7 10.1 %all-to-all-done.1 = f32[24,9,128]{2,1,0:T(8,128)S(1)} async-done(((f32[24,9,128]{2,1,0:T(8,128)}), f32[24,9,128]{2,1,0:T(8,128)S(1)}, u32[]{:S(2)}, u32[]{:S(2)}) %all-to-all-start.1) | async-done | bytes 110624 | tf_op jit(solution)/shard_map/sums_and_lists/all_to_all | solution.py:187
  32.7 0.0 copy-start.1
  32.7 4.8 %all-to-all-start = ((bf16[24,32,1024]{2,1,0:T(8,128)(2,1)}), bf16[24,32,1024]{2,1,0:T(8,128)(2,1)S(1)}, u32[]{:S(2)}, u32[]{:S(2)}) async-start(bf16[24,32,1024]{2,1,0:T(8,128)(2,1)} %bitcast.18), calls=%async_computation | async-start | bytes 3145728 | tf_op jit(solution)/shard_map/slabs_out/all_to_all | solution.py:187
  37.6 0.0 copy-done.1
  37.7 0.1 select_reduce_fusion.1
  37.8 0.1 copy.9
  37.9 0.1 copy.10
  38.0 0.2 fusion
  38.1 0.4 select_reduce_fusion
  38.5 0.5 select_reduce_fusion.2
  39.0 0.3 and_reduce_fusion
  39.3 0.1 copy.12
  39.4 0.0 copy-start
  39.4 0.1 copy.11
  39.5 0.2 broadcast_in_dim.62
  39.7 0.2 reshape.67
  39.9 0.2 broadcast_in_dim.63
  40.1 0.2 reshape.70
  40.4 9.1 %psum.14 = f32[8,128]{1,0:T(8,128)S(1)} all-reduce(f32[8,128]{1,0:T(8,128)S(1)} %slice_reduce_fusion), channel_id=1, replica_groups=mesh['z'=12,'core'=2,'y'=8,'x'=4] {'x'}, use_global_device_ids=true, to_apply=%region_1.0 | all-reduce | flops 1024 | bytes 8192 | tf_op jit(solution)/shard_map/feature_scale/psum | solution.py:222
  49.5 15.0 %psum.15 = f32[8,128]{1,0:T(8,128)S(1)} all-reduce(f32[8,128]{1,0:T(8,128)S(1)} %psum.14), channel_id=1, replica_groups=mesh['z'=12,'core'=2,'y'=8,'x'=4] {'y'}, use_global_device_ids=true, to_apply=%region_2.0 | all-reduce | flops 1024 | bytes 8192 | tf_op jit(solution)/shard_map/feature_scale/psum | solution.py:222
  64.5 29.5 %all-to-all-done = bf16[24,32,1024]{2,1,0:T(8,128)(2,1)S(1)} async-done(((bf16[24,32,1024]{2,1,0:T(8,128)(2,1)}), bf16[24,32,1024]{2,1,0:T(8,128)(2,1)S(1)}, u32[]{:S(2)}, u32[]{:S(2)}) %all-to-all-start) | async-done | bytes 1572896 | tf_op jit(solution)/shard_map/slabs_out/all_to_all | solution.py:187
  94.0 0.0 copy-done
  94.0 0.9 first_logits.1
  95.0 16.4 %all_to_all.20.refs_0_ = f32[24,8,128]{2,1,0:T(8,128)S(1)} all-to-all(f32[24,8,128]{2,1,0:T(8,128)S(1)} %get-tuple-element.9), channel_id=1, replica_groups=mesh['z'=12,'core'=2,'y'=8,'x'=4] {'z','core'}, dimensions={0} | all-to-all | bytes 196608 | tf_op jit(solution)/shard_map/stats_out/all_to_all | solution.py:187
  111.4 1.8 %middle_update.1 = (f32[256,1024]{1,0:T(8,128)S(1)}, f32[256,768]{1,0:T(8,128)S(1)}, f32[24,8,128]{2,1,0:T(8,128)S(1)}) custom-call(f32[24,8,128]{2,1,0:T(8,128)S(1)} %all_to_all.20.refs_0_, f32[24,8,128]{2,1,0:T(8,128)S(1)} %pad.7.same_ref.refs_1_, f32[24,8,128]{2,1,0:T(8,128)S(1)} %pad.8.swap_ref.refs_2_, ...), custom_call_target="tpu_custom_call" | custom-call | flops 1207959552 | bytes 5242880 | tf_op jit(solution)/shard_map/middle_update/pallas_call | solution.py:267
  113.2 14.7 %all_to_all.21.refs_0_ = f32[24,8,128]{2,1,0:T(8,128)S(1)} all-to-all(f32[24,8,128]{2,1,0:T(8,128)S(1)} %get-tuple-element.11), channel_id=1, replica_groups=mesh['z'=12,'core'=2,'y'=8,'x'=4] {'z','core'}, dimensions={0} | all-to-all | bytes 196608 | tf_op jit(solution)/shard_map/last_stats_out/all_to_all | solution.py:187
  127.8 1.8 %last_update.1 = (f32[256,1024]{1,0:T(8,128)}, f32[1,256]{1,0:T(1,128)}) custom-call(f32[24,8,128]{2,1,0:T(8,128)S(1)} %all_to_all.21.refs_0_, f32[24,8,128]{2,1,0:T(8,128)S(1)} %pad.7.same_ref.refs_1_, f32[24,8,128]{2,1,0:T(8,128)S(1)} %pad.8.swap_ref.refs_2_, f32[256,768]{1,0:T(8,128)S(1)} %get-tuple-element.12.refs_3_, ...), custom_call_target="tpu_custom_call" | custom-call | flops 402653184 | bytes 5242880 | tf_op jit(solution)/shard_map/last_update/pallas_call | solution.py:277
  (11 shorter events, 0.1 us)
Async XLA Ops:
  2.3 30.4 %all-to-all-start.1 = ((f32[24,9,128]{2,1,0:T(8,128)}), f32[24,9,128]{2,1,0:T(8,128)S(1)}, u32[]{:S(2)}, u32[]{:S(2)}) async-start(f32[24,9,128]{2,1,0:T(8,128)} %sums_and_lists.1), calls=%async_computation.1 | async-start | bytes 393216 | tf_op jit(solution)/shard_map/sums_and_lists/all_to_all | solution.py:187
  32.7 4.9 %copy-start.1 = (s32[1,24]{1,0:T(1,128)S(1)}, s32[1,24]{1,0:T(1,128)}, u32[]{:S(2)}) copy-start(s32[1,24]{1,0:T(1,128)} %refs_1_.1) | copy-start | bytes 292
  32.7 61.3 %all-to-all-start = ((bf16[24,32,1024]{2,1,0:T(8,128)(2,1)}), bf16[24,32,1024]{2,1,0:T(8,128)(2,1)S(1)}, u32[]{:S(2)}, u32[]{:S(2)}) async-start(bf16[24,32,1024]{2,1,0:T(8,128)(2,1)} %bitcast.18), calls=%async_computation | async-start | bytes 3145728 | tf_op jit(solution)/shard_map/slabs_out/all_to_all | solution.py:187
  39.4 54.6 %copy-start = (bf16[1,1,256,1024]{3,2,1,0:T(8,128)(2,1)S(1)}, bf16[1,1,256,1024]{3,2,1,0:T(8,128)(2,1)}, u32[]{:S(2)}) copy-start(bf16[1,1,256,1024]{3,2,1,0:T(8,128)(2,1)} %param.7) | copy-start | bytes 1572868

commit v4 on v3

--- a/solution.py
+++ b/solution.py
@@ -34,12 +34,14 @@
     listed, slabs = lists_ref.shape
     wide = emb_ref[...].astype(jnp.float32)
     squares = jnp.sum(wide * wide, axis=0, keepdims=True)
-    lines = [squares[:, c : c + LANES] for c in range(0, wide.shape[1], LANES)]
     lane = lax.broadcasted_iota(jnp.int32, (1, LANES), 1)
     names = jnp.zeros((1, LANES), jnp.int32)
     for n in range(slabs * listed):
         names = jnp.where(lane == n, lists_ref[n % listed, n // listed], names)
-    payload = jnp.concatenate([*lines, names.astype(jnp.float32)], axis=0)
+    half = wide.shape[1] // 2
+    upper = jnp.concatenate([squares[:, :half], names.astype(jnp.float32)], axis=1)
+    lower = jnp.concatenate([squares[:, half:], jnp.zeros((1, LANES), jnp.float32)], axis=1)
+    payload = jnp.concatenate([upper, lower], axis=0).astype(jnp.bfloat16)
     for p in range(out_ref.shape[0]):
         out_ref[p] = payload
 
@@ -94,18 +96,15 @@
 
 
 def block_stats(block_low, std_ref, stat_ref, logits_ref=None):
-    peers, rows, lanes = stat_ref.shape
     lines = []
     for c, chunk, logits in block_logits(block_low, std_ref):
         if logits_ref is not None:
             logits_ref[:, c : c + chunk] = logits
         largest = jnp.max(logits, axis=0, keepdims=True)
         total = jnp.sum(jnp.exp(logits - largest), axis=0, keepdims=True)
-        both = largest + jnp.log(total)
-        lines += [both[:, h * lanes : (h + 1) * lanes] for h in range(2)]
-    lines += [jnp.zeros((1, lanes), jnp.float32)] * (rows - len(lines))
-    stat = jnp.concatenate(lines, axis=0)
-    for p in range(peers):
+        lines.append(largest + jnp.log(total))
+    stat = jnp.concatenate(lines, axis=1)
+    for p in range(stat_ref.shape[0]):
         stat_ref[p] = stat
 
 
@@ -119,29 +118,27 @@
 
 
 def combine(stats_ref, same_ref, swap_ref, slab_rows):
-    peers, rows, lanes = stats_ref.shape
-    own = stats_ref[...].reshape(peers * rows, lanes)
-    lane = lax.broadcasted_iota(jnp.int32, own.shape, 1)
-    ahead = pltpu.roll(own, lanes - slab_rows, 1)
-    behind = pltpu.roll(own, slab_rows, 1)
-    other = jnp.where(lane % (2 * slab_rows) < slab_rows, ahead, behind)
-    own = own.reshape(peers, rows, lanes)
-    other = other.reshape(peers, rows, lanes)
-    first = jnp.where(same_ref[...] > 0, own, -jnp.inf)
-    second = jnp.where(swap_ref[...] > 0, other, -jnp.inf)
-    summit = jnp.max(jnp.maximum(first, second), axis=0)
-    live = summit > -jnp.inf
-    summit = jnp.where(live, summit, 0.0)
-    total = jnp.sum(jnp.exp(first - summit) + jnp.exp(second - summit), axis=0)
-    return jnp.where(live, summit + jnp.log(jnp.where(live, total, 1.0)), jnp.inf)
+    lines = []
+    for c in range(0, stats_ref.shape[2], LANES):
+        own = stats_ref[:, 0, c : c + LANES]
+        lane = lax.broadcasted_iota(jnp.int32, own.shape, 1)
+        ahead = pltpu.roll(own, LANES - slab_rows, 1)
+        behind = pltpu.roll(own, slab_rows, 1)
+        other = jnp.where(lane % (2 * slab_rows) < slab_rows, ahead, behind)
+        first = jnp.where(same_ref[:, c : c + LANES] > 0, own, -jnp.inf)
+        second = jnp.where(swap_ref[:, c : c + LANES] > 0, other, -jnp.inf)
+        summit = jnp.max(jnp.maximum(first, second), axis=0, keepdims=True)
+        live = summit > -jnp.inf
+        summit = jnp.where(live, summit, 0.0)
+        total = jnp.sum(jnp.exp(first - summit) + jnp.exp(second - summit), axis=0, keepdims=True)
+        lines.append(jnp.where(live, summit + jnp.log(jnp.where(live, total, 1.0)), jnp.inf))
+    return jnp.concatenate(lines, axis=1)
 
 
 def update(normal, logits, std_ref, old):
     parts = []
     for c, chunk, values in logits:
-        for h in range(0, chunk, LANES):
-            r = (c + h) // LANES
-            parts.append(jnp.exp(values[:, h : h + LANES] - normal[r : r + 1, :]))
+        parts.append(jnp.exp(values - normal[:, c : c + chunk]))
     resp = jnp.concatenate(parts, axis=1)
     weight = jnp.sum(resp, axis=1, keepdims=True)
     sums = lax.dot_general(
@@ -201,7 +198,7 @@
         lists = coarse_lists.T
         payload = pl.pallas_call(
             share_body,
-            out_shape=jax.ShapeDtypeStruct((peers, width // LANES + 1, LANES), f32),
+            out_shape=jax.ShapeDtypeStruct((peers, 2, width // 2 + LANES), jnp.bfloat16),
             in_specs=[pl.BlockSpec(memory_space=pltpu.SMEM)] + vmem(1),
             out_specs=vmem(1)[0],
         )(lists, embeddings)
@@ -218,14 +215,14 @@
         received = spread(outgoing.reshape(peers, most * slab_rows, width)).reshape(slots, width)
 
     with jax.named_scope("feature_scale"):
-        total = jnp.sum(shared[:, : width // LANES], axis=0)
+        total = jnp.sum(shared[:, :, : width // 2].astype(f32), axis=0).reshape(-1, LANES)
         total = lax.psum(lax.psum(total, "x"), "y")
         scale = lax.rsqrt(total / total_rows + 1e-06)
 
     with jax.named_scope("slot_masks"):
         me = lax.axis_index(DP)
         ids = jnp.arange(peers, dtype=jnp.int32)
-        lists_all = shared[:, width // LANES, : slabs * listed].astype(jnp.int32)
+        lists_all = shared[:, 0, width // 2 : width // 2 + slabs * listed].astype(jnp.int32)
         home_of = jnp.sum(jnp.where(lists_all[:, :, None] == ids, home[0], 0), axis=2)
         hits = jnp.any(home_of.reshape(peers, slabs, listed)[..., None] == ids, axis=2)
         order = jnp.arange(slabs)
@@ -240,16 +237,14 @@
             found = chosen[..., None] & (place[:, None] == wanted[:, None, None])
             found = jnp.any(found, axis=2).astype(f32)
             found = found.transpose(2, 0, 1).reshape(peers, peers * most)
-            found = jnp.repeat(found, slab_rows, axis=1).reshape(peers, -1, LANES)
-            return jnp.pad(found, ((0, 0), (0, -found.shape[1] % 8), (0, 0)))
+            return jnp.repeat(found, slab_rows, axis=1)
 
         same, swap = lanes_of(turn), lanes_of(1 - turn)
 
     block = centroids[0, 0]
-    rows_of_stat = same.shape[1]
     work = 2 * slots * block.shape[0] * width
     logits_shape = jax.ShapeDtypeStruct((block.shape[0], slots), f32)
-    stat_shape = jax.ShapeDtypeStruct((peers, rows_of_stat, LANES), f32)
+    stat_shape = jax.ShapeDtypeStruct((peers, 1, slots), f32)
     block_shape = jax.ShapeDtypeStruct(block.shape, f32)
     with jax.named_scope("first_logits"):
         std, stat = call(

time: 130 us -> 125 us (0.962)
  waiting for transfers between devices: 39.6 us -> 36 us
    all_to_all x2, waiting for transfers between devices: 39.6 us -> 36 us  [spread(): return lax.all_to_all(x, DP, split_axis=0, concat_axis=0, tiled=True)]
where the time goes in v4:
time: 125 us; the launch traced here: 124 us
  blocking collectives  54 us (43%)
  waiting for transfers between devices  36 us (29%)
  starting transfers between devices  21.1 us (17%)
  Pallas kernels  9.75 us (8%)
  other arithmetic  1.55 us (1%)
  local copies, waits for them, and re-layouts  1.26 us (1%)
    all_to_all x2, waiting for transfers between devices, spread(): return lax.all_to_all(x, DP, split_axis=0, concat_axis=0, tiled=True)  36 us
    all_to_all x2, blocking collectives, spread(): return lax.all_to_all(x, DP, split_axis=0, concat_axis=0, tiled=True)  29.9 us
    psum x2, blocking collectives, per_device(): total = lax.psum(lax.psum(total, 'x'), 'y')  24.1 us
    all_to_all x2, starting transfers between devices, spread(): return lax.all_to_all(x, DP, split_axis=0, concat_axis=0, tiled=True)  21.1 us
    pallas_call x1, Pallas kernels, per_device(): pl.pallas_call(lambda *refs: dispatch(slab_rows, most, peers, *refs), out...  3.67 us
  transfers between devices with their start and end apart: 2, of which 2 were waited for; matrix products, arithmetic and copies ran while one was open for 2% of the time, Pallas kernels for 3%

profile of v4, /device:TPU:1, one launch (start us, length us, event | category | flops | bytes accessed | tf_op | source)
XLA Modules:
  0.0 124.4 jit_solution(8610970118432505525)
XLA Ops:
  0.6 1.6 %sums_and_lists.1 = bf16[24,2,640]{2,1,0:T(2,128)(2,1)} custom-call(s32[4,8]{1,0:T(4,128)} %bitcast.23, bf16[128,1024]{1,0:T(8,128)(2,1)} %emb_ref.1), custom_call_target="tpu_custom_call" | custom-call | tf_op jit(solution)/shard_map/sums_and_lists/pallas_call | solution.py:199
  2.3 16.7 %all-to-all-start.1 = ((bf16[24,2,640]{2,1,0:T(2,128)(2,1)}), bf16[24,2,640]{2,1,0:T(2,128)(2,1)S(1)}, u32[]{:S(2)}, u32[]{:S(2)}) async-start(bf16[24,2,640]{2,1,0:T(2,128)(2,1)} %sums_and_lists.1), calls=%async_computation.1 | async-start | bytes 122880 | tf_op jit(solution)/shard_map/sums_and_lists/all_to_all | solution.py:184
  19.0 3.7 %slabs_out.1 = bf16[768,1024]{1,0:T(8,128)(2,1)} custom-call(s32[4,8]{1,0:T(4,128)} %bitcast.24, s32[1,24]{1,0:T(1,128)} %refs_1_.1, bf16[128,1024]{1,0:T(8,128)(2,1)} %emb_ref.1), custom_call_target="tpu_custom_call" | custom-call | tf_op jit(solution)/shard_map/slabs_out/pallas_call | solution.py:208
  22.6 6.6 %all-to-all-done.1 = bf16[24,2,640]{2,1,0:T(2,128)(2,1)S(1)} async-done(((bf16[24,2,640]{2,1,0:T(2,128)(2,1)}), bf16[24,2,640]{2,1,0:T(2,128)(2,1)S(1)}, u32[]{:S(2)}, u32[]{:S(2)}) %all-to-all-start.1) | async-done | bytes 61472 | tf_op jit(solution)/shard_map/sums_and_lists/all_to_all | solution.py:184
  29.2 0.0 copy-start.1
  29.2 4.4 %all-to-all-start = ((bf16[24,32,1024]{2,1,0:T(8,128)(2,1)}), bf16[24,32,1024]{2,1,0:T(8,128)(2,1)S(1)}, u32[]{:S(2)}, u32[]{:S(2)}) async-start(bf16[24,32,1024]{2,1,0:T(8,128)(2,1)} %bitcast.18), calls=%async_computation | async-start | bytes 3145728 | tf_op jit(solution)/shard_map/slabs_out/all_to_all | solution.py:184
  33.7 0.1 convert_reduce_fusion
  33.7 0.0 copy-done.1
  33.7 0.1 select_reduce_fusion.1
  33.9 0.1 copy.9
  34.0 0.1 copy.10
  34.1 0.2 fusion
  34.2 0.4 select_reduce_fusion
  34.6 0.0 copy-start
  34.6 0.5 select_reduce_fusion.2
  35.1 0.3 and_reduce_fusion
  35.4 0.1 copy.12
  35.5 0.1 copy.11
  35.6 0.2 broadcast_in_dim.62
  35.8 0.3 reshape.72.same_ref.refs_1_
  36.0 0.2 broadcast_in_dim.63
  36.3 0.3 reshape.75.swap_ref.refs_2_
  36.5 9.1 %psum.14 = f32[8,128]{1,0:T(8,128)S(1)} all-reduce(f32[8,128]{1,0:T(8,128)S(1)} %reshape.69), channel_id=1, replica_groups=mesh['z'=12,'core'=2,'y'=8,'x'=4] {'x'}, use_global_device_ids=true, to_apply=%region_1.0 | all-reduce | flops 1024 | bytes 8192 | tf_op jit(solution)/shard_map/feature_scale/psum | solution.py:219
  45.6 15.0 %psum.15 = f32[8,128]{1,0:T(8,128)S(1)} all-reduce(f32[8,128]{1,0:T(8,128)S(1)} %psum.14), channel_id=1, replica_groups=mesh['z'=12,'core'=2,'y'=8,'x'=4] {'y'}, use_global_device_ids=true, to_apply=%region_2.0 | all-reduce | flops 1024 | bytes 8192 | tf_op jit(solution)/shard_map/feature_scale/psum | solution.py:219
  60.7 29.4 %all-to-all-done = bf16[24,32,1024]{2,1,0:T(8,128)(2,1)S(1)} async-done(((bf16[24,32,1024]{2,1,0:T(8,128)(2,1)}), bf16[24,32,1024]{2,1,0:T(8,128)(2,1)S(1)}, u32[]{:S(2)}, u32[]{:S(2)}) %all-to-all-start) | async-done | bytes 1572896 | tf_op jit(solution)/shard_map/slabs_out/all_to_all | solution.py:184
  90.0 0.0 copy-done
  90.0 0.9 first_logits.1
  91.0 15.9 %all_to_all.20.refs_0_ = f32[24,1,768]{2,1,0:T(1,128)S(1)} all-to-all(f32[24,1,768]{2,1,0:T(1,128)S(1)} %get-tuple-element.9), channel_id=1, replica_groups=mesh['z'=12,'core'=2,'y'=8,'x'=4] {'z','core'}, dimensions={0} | all-to-all | bytes 147456 | tf_op jit(solution)/shard_map/stats_out/all_to_all | solution.py:184
  106.9 1.8 %middle_update.1 = (f32[256,1024]{1,0:T(8,128)S(1)}, f32[256,768]{1,0:T(8,128)S(1)}, f32[24,1,768]{2,1,0:T(1,128)S(1)}) custom-call(f32[24,1,768]{2,1,0:T(1,128)S(1)} %all_to_all.20.refs_0_, f32[24,768]{1,0:T(8,128)S(1)} %reshape.72.same_ref.refs_1_, f32[24,768]{1,0:T(8,128)S(1)} %reshape.75.swap_ref.refs_2_, ...), custom_call_target="tpu_custom_call" | custom-call | flops 1207959552 | bytes 5242880 | tf_op jit(solution)/shard_map/middle_update/pallas_call | solution.py:262
  108.7 14.0 %all_to_all.21.refs_0_ = f32[24,1,768]{2,1,0:T(1,128)S(1)} all-to-all(f32[24,1,768]{2,1,0:T(1,128)S(1)} %get-tuple-element.11), channel_id=1, replica_groups=mesh['z'=12,'core'=2,'y'=8,'x'=4] {'z','core'}, dimensions={0} | all-to-all | bytes 147456 | tf_op jit(solution)/shard_map/last_stats_out/all_to_all | solution.py:184
  122.7 1.7 %last_update.1 = (f32[256,1024]{1,0:T(8,128)}, f32[1,256]{1,0:T(1,128)}) custom-call(f32[24,1,768]{2,1,0:T(1,128)S(1)} %all_to_all.21.refs_0_, f32[24,768]{1,0:T(8,128)S(1)} %reshape.72.same_ref.refs_1_, f32[24,768]{1,0:T(8,128)S(1)} %reshape.75.swap_ref.refs_2_, f32[256,768]{1,0:T(8,128)S(1)} %get-tuple-element.12.refs_3_, ...), custom_call_target="tpu_custom_call" | custom-call | flops 402653184 | bytes 5242880 | tf_op jit(solution)/shard_map/last_update/pallas_call | solution.py:272
  (9 shorter events, 0.1 us)
Async XLA Ops:
  2.3 27.0 %all-to-all-start.1 = ((bf16[24,2,640]{2,1,0:T(2,128)(2,1)}), bf16[24,2,640]{2,1,0:T(2,128)(2,1)S(1)}, u32[]{:S(2)}, u32[]{:S(2)}) async-start(bf16[24,2,640]{2,1,0:T(2,128)(2,1)} %sums_and_lists.1), calls=%async_computation.1 | async-start | bytes 122880 | tf_op jit(solution)/shard_map/sums_and_lists/all_to_all | solution.py:184
  29.2 4.5 %copy-start.1 = (s32[1,24]{1,0:T(1,128)S(1)}, s32[1,24]{1,0:T(1,128)}, u32[]{:S(2)}) copy-start(s32[1,24]{1,0:T(1,128)} %refs_1_.1) | copy-start | bytes 292
  29.2 60.8 %all-to-all-start = ((bf16[24,32,1024]{2,1,0:T(8,128)(2,1)}), bf16[24,32,1024]{2,1,0:T(8,128)(2,1)S(1)}, u32[]{:S(2)}, u32[]{:S(2)}) async-start(bf16[24,32,1024]{2,1,0:T(8,128)(2,1)} %bitcast.18), calls=%async_computation | async-start | bytes 3145728 | tf_op jit(solution)/shard_map/slabs_out/all_to_all | solution.py:184
  34.6 55.4 %copy-start = (bf16[1,1,256,1024]{3,2,1,0:T(8,128)(2,1)S(1)}, bf16[1,1,256,1024]{3,2,1,0:T(8,128)(2,1)}, u32[]{:S(2)}) copy-start(bf16[1,1,256,1024]{3,2,1,0:T(8,128)(2,1)} %param.7) | copy-start | bytes 1572868

commit v5 on v4

--- a/solution.py
+++ b/solution.py
@@ -30,7 +30,7 @@
     )
 
 
-def share_body(lists_ref, emb_ref, out_ref):
+def share_body(cores, lists_ref, emb_ref, out_ref):
     listed, slabs = lists_ref.shape
     wide = emb_ref[...].astype(jnp.float32)
     squares = jnp.sum(wide * wide, axis=0, keepdims=True)
@@ -38,12 +38,15 @@
     names = jnp.zeros((1, LANES), jnp.int32)
     for n in range(slabs * listed):
         names = jnp.where(lane == n, lists_ref[n % listed, n // listed], names)
-    half = wide.shape[1] // 2
-    upper = jnp.concatenate([squares[:, :half], names.astype(jnp.float32)], axis=1)
-    lower = jnp.concatenate([squares[:, half:], jnp.zeros((1, LANES), jnp.float32)], axis=1)
-    payload = jnp.concatenate([upper, lower], axis=0).astype(jnp.bfloat16)
-    for p in range(out_ref.shape[0]):
-        out_ref[p] = payload
+    part = wide.shape[1] // (2 * cores)
+    names = names.astype(jnp.float32)
+    for core in range(cores):
+        at = 2 * part * core
+        upper = jnp.concatenate([squares[:, at : at + part], names], axis=1)
+        lower = jnp.concatenate([squares[:, at + part : at + 2 * part], names], axis=1)
+        payload = jnp.concatenate([upper, lower], axis=0).astype(jnp.bfloat16)
+        for p in range(core, out_ref.shape[0], cores):
+            out_ref[p] = payload
 
 
 def dispatch(slab_rows, most, peers, lists_ref, home_ref, emb_ref, out_ref, table):
@@ -108,13 +111,15 @@
         stat_ref[p] = stat
 
 
-def first_body(got_ref, scale_ref, block_ref, same_ref, swap_ref, std_ref, stat_ref):
+def first_body(
+    got_ref, scale_ref, block_ref, same_ref, swap_ref, std_ref, logits_ref, stat_ref
+):
     chunk = 2 * LANES
     scale = jnp.concatenate([scale_ref[r : r + 1, :] for r in range(scale_ref.shape[0])], axis=1)
     for c in range(got_ref.shape[0] // chunk):
         at = slice(c * chunk, (c + 1) * chunk)
         std_ref[at, :] = (got_ref[at, :].astype(jnp.float32) * scale).astype(jnp.bfloat16)
-    block_stats(block_ref[...], std_ref, stat_ref)
+    block_stats(block_ref[...], std_ref, stat_ref, logits_ref)
 
 
 def combine(stats_ref, same_ref, swap_ref, slab_rows):
@@ -155,6 +160,7 @@
     stats_ref,
     same_ref,
     swap_ref,
+    logits_ref,
     std_ref,
     old_ref,
     new_ref,
@@ -163,7 +169,7 @@
 ):
     normal = combine(stats_ref, same_ref, swap_ref, slab_rows)
     old = old_ref[...]
-    logits = block_logits(old.astype(jnp.bfloat16), std_ref)
+    logits = [(0, logits_ref.shape[1], logits_ref[...])]
     current, _ = update(normal, logits, std_ref, old.astype(jnp.float32))
     new_ref[...] = current
     block_stats(current.astype(jnp.bfloat16), std_ref, stat_ref, next_ref)
@@ -191,14 +197,16 @@
     slabs, listed = coarse_lists.shape
     slab_rows = row_count // slabs
     most = 2
+    cores = lax.axis_size(DP[1])
+    part = width // (2 * cores)
     slots = peers * most * slab_rows
     f32 = jnp.float32
 
     with jax.named_scope("sums_and_lists"):
         lists = coarse_lists.T
         payload = pl.pallas_call(
-            share_body,
-            out_shape=jax.ShapeDtypeStruct((peers, 2, width // 2 + LANES), jnp.bfloat16),
+            lambda *refs: share_body(cores, *refs),
+            out_shape=jax.ShapeDtypeStruct((peers, 2, part + LANES), jnp.bfloat16),
             in_specs=[pl.BlockSpec(memory_space=pltpu.SMEM)] + vmem(1),
             out_specs=vmem(1)[0],
         )(lists, embeddings)
@@ -215,14 +223,15 @@
         received = spread(outgoing.reshape(peers, most * slab_rows, width)).reshape(slots, width)
 
     with jax.named_scope("feature_scale"):
-        total = jnp.sum(shared[:, :, : width // 2].astype(f32), axis=0).reshape(-1, LANES)
+        total = jnp.sum(shared[:, :, :part].astype(f32), axis=0).reshape(-1, LANES)
         total = lax.psum(lax.psum(total, "x"), "y")
+        total = lax.all_gather(total, DP[1], tiled=True)
         scale = lax.rsqrt(total / total_rows + 1e-06)
 
     with jax.named_scope("slot_masks"):
         me = lax.axis_index(DP)
         ids = jnp.arange(peers, dtype=jnp.int32)
-        lists_all = shared[:, 0, width // 2 : width // 2 + slabs * listed].astype(jnp.int32)
+        lists_all = shared[:, 0, part : part + slabs * listed].astype(jnp.int32)
         home_of = jnp.sum(jnp.where(lists_all[:, :, None] == ids, home[0], 0), axis=2)
         hits = jnp.any(home_of.reshape(peers, slabs, listed)[..., None] == ids, axis=2)
         order = jnp.arange(slabs)
@@ -247,9 +256,9 @@
     stat_shape = jax.ShapeDtypeStruct((peers, 1, slots), f32)
     block_shape = jax.ShapeDtypeStruct(block.shape, f32)
     with jax.named_scope("first_logits"):
-        std, stat = call(
+        std, logits, stat = call(
             first_body,
-            (jax.ShapeDtypeStruct((slots, width), jnp.bfloat16), stat_shape),
+            (jax.ShapeDtypeStruct((slots, width), jnp.bfloat16), logits_shape, stat_shape),
             vmem(5),
             work,
             4 << 20,
@@ -262,10 +271,10 @@
             old, logits, stat = call(
                 lambda *refs: middle_body(slab_rows, *refs),
                 (block_shape, logits_shape, stat_shape),
-                vmem(5),
-                3 * work,
+                vmem(6),
+                2 * work,
                 5 << 20,
-            )(stats, same, swap, std, old)
+            )(stats, same, swap, logits, std, old)
     with jax.named_scope("last_stats_out"):
         stats = spread(stat)
     with jax.named_scope("last_update"):

time: 125 us -> 124 us (level)
  waiting for transfers between devices: 36 us -> 29.9 us
  blocking collectives: 54 us -> 59.8 us
    all_to_all x2, waiting for transfers between devices: 36 us -> 29.9 us  [spread(): return lax.all_to_all(x, DP, split_axis=0, concat_axis=0, tiled=True)]
    all_gather x0 -> x1, blocking collectives: none -> 5.77 us  [per_device(): total = lax.all_gather(total, DP[1], tiled=True)]
where the time goes in v5:
time: 124 us
  blocking collectives  59.8 us (48%)
  waiting for transfers between devices  29.9 us (24%)
  starting transfers between devices  21 us (17%)
  Pallas kernels  9.3 us (8%)
  other arithmetic  1.53 us (1%)
  local copies, waits for them, and re-layouts  1.26 us (1%)
    all_to_all x2, blocking collectives, spread(): return lax.all_to_all(x, DP, split_axis=0, concat_axis=0, tiled=True)  29.9 us
    all_to_all x2, waiting for transfers between devices, spread(): return lax.all_to_all(x, DP, split_axis=0, concat_axis=0, tiled=True)  29.9 us
    psum x2, blocking collectives, per_device(): total = lax.psum(lax.psum(total, 'x'), 'y')  24.1 us
    all_to_all x2, starting transfers between devices, spread(): return lax.all_to_all(x, DP, split_axis=0, concat_axis=0, tiled=True)  21 us
    all_gather x1, blocking collectives, per_device(): total = lax.all_gather(total, DP[1], tiled=True)  5.77 us
    pallas_call x1, Pallas kernels, per_device(): pl.pallas_call(lambda *refs: dispatch(slab_rows, most, peers, *refs), out...  3.67 us
  transfers between devices with their start and end apart: 2, of which 2 were waited for; matrix products, arithmetic and copies ran while one was open for 2% of the time, Pallas kernels for 3%

profile of v5, /device:TPU:1, one launch (start us, length us, event | category | flops | bytes accessed | tf_op | source)
XLA Modules:
  0.0 123.5 jit_solution(4032884727296123657)
XLA Ops:
  0.6 1.6 %sums_and_lists.1 = bf16[24,2,384]{2,1,0:T(2,128)(2,1)} custom-call(s32[4,8]{1,0:T(4,128)} %bitcast.26, bf16[128,1024]{1,0:T(8,128)(2,1)} %refs_1_.3), custom_call_target="tpu_custom_call" | custom-call | tf_op jit(solution)/shard_map/sums_and_lists/pallas_call | solution.py:207
  2.3 16.7 %all-to-all-start.1 = ((bf16[24,2,384]{2,1,0:T(2,128)(2,1)}), bf16[24,2,384]{2,1,0:T(2,128)(2,1)S(1)}, u32[]{:S(2)}, u32[]{:S(2)}) async-start(bf16[24,2,384]{2,1,0:T(2,128)(2,1)} %sums_and_lists.1), calls=%async_computation.1 | async-start | bytes 73728 | tf_op jit(solution)/shard_map/sums_and_lists/all_to_all | solution.py:190
  19.0 3.7 %slabs_out.1 = bf16[768,1024]{1,0:T(8,128)(2,1)} custom-call(s32[4,8]{1,0:T(4,128)} %bitcast.27, s32[1,24]{1,0:T(1,128)} %refs_1_.2, bf16[128,1024]{1,0:T(8,128)(2,1)} %refs_1_.3), custom_call_target="tpu_custom_call" | custom-call | tf_op jit(solution)/shard_map/slabs_out/pallas_call | solution.py:216
  22.6 6.2 %all-to-all-done.1 = bf16[24,2,384]{2,1,0:T(2,128)(2,1)S(1)} async-done(((bf16[24,2,384]{2,1,0:T(2,128)(2,1)}), bf16[24,2,384]{2,1,0:T(2,128)(2,1)S(1)}, u32[]{:S(2)}, u32[]{:S(2)}) %all-to-all-start.1) | async-done | bytes 36896 | tf_op jit(solution)/shard_map/sums_and_lists/all_to_all | solution.py:190
  28.8 0.0 copy-start.1
  28.8 4.3 %all-to-all-start = ((bf16[24,32,1024]{2,1,0:T(8,128)(2,1)}), bf16[24,32,1024]{2,1,0:T(8,128)(2,1)S(1)}, u32[]{:S(2)}, u32[]{:S(2)}) async-start(bf16[24,32,1024]{2,1,0:T(8,128)(2,1)} %bitcast.21), calls=%async_computation | async-start | bytes 3145728 | tf_op jit(solution)/shard_map/slabs_out/all_to_all | solution.py:190
  33.3 0.0 copy-done.1
  33.3 0.1 select_reduce_fusion.1
  33.4 0.1 copy.12
  33.5 0.1 copy.13
  33.6 0.2 fusion
  33.8 0.4 select_reduce_fusion
  34.1 0.0 copy-start
  34.1 0.5 select_reduce_fusion.2
  34.7 0.3 and_reduce_fusion
  34.9 0.1 copy.15
  35.0 0.1 copy.14
  35.1 0.2 broadcast_in_dim.62
  35.3 0.3 reshape.72.same_ref.refs_1_
  35.6 0.2 broadcast_in_dim.63
  35.8 0.3 reshape.75.swap_ref.refs_2_
  36.1 9.1 %psum.14 = f32[4,128]{1,0:T(4,128)S(1)} all-reduce(f32[4,128]{1,0:T(4,128)S(1)} %reshape.69), channel_id=1, replica_groups=mesh['z'=12,'core'=2,'y'=8,'x'=4] {'x'}, use_global_device_ids=true, to_apply=%region_1.0 | all-reduce | flops 512 | bytes 4096 | tf_op jit(solution)/shard_map/feature_scale/psum | solution.py:227
  45.1 15.0 %psum.15 = f32[4,128]{1,0:T(4,128)S(1)} all-reduce(f32[4,128]{1,0:T(4,128)S(1)} %psum.14), channel_id=1, replica_groups=mesh['z'=12,'core'=2,'y'=8,'x'=4] {'y'}, use_global_device_ids=true, to_apply=%region_2.0 | all-reduce | flops 512 | bytes 4096 | tf_op jit(solution)/shard_map/feature_scale/psum | solution.py:227
  60.2 5.8 %all-gather = f32[2,4,128]{2,1,0:T(4,128)S(1)} all-gather(f32[1,4,128]{2,1,0:T(4,128)S(1)} %bitcast.28), channel_id=1, replica_groups=mesh['z'=12,'core'=2,'y'=8,'x'=4] {'core'}, dimensions={0}, use_global_device_ids=true | all-gather | bytes 6144 | tf_op jit(solution)/shard_map/feature_scale/all_gather | solution.py:228
  65.9 23.7 %all-to-all-done = bf16[24,32,1024]{2,1,0:T(8,128)(2,1)S(1)} async-done(((bf16[24,32,1024]{2,1,0:T(8,128)(2,1)}), bf16[24,32,1024]{2,1,0:T(8,128)(2,1)S(1)}, u32[]{:S(2)}, u32[]{:S(2)}) %all-to-all-start) | async-done | bytes 1572896 | tf_op jit(solution)/shard_map/slabs_out/all_to_all | solution.py:190
  89.6 0.0 copy-done
  89.6 0.9 first_logits.1
  90.5 15.9 %all_to_all.20.refs_0_ = f32[24,1,768]{2,1,0:T(1,128)S(1)} all-to-all(f32[24,1,768]{2,1,0:T(1,128)S(1)} %get-tuple-element.10), channel_id=1, replica_groups=mesh['z'=12,'core'=2,'y'=8,'x'=4] {'z','core'}, dimensions={0} | all-to-all | bytes 147456 | tf_op jit(solution)/shard_map/stats_out/all_to_all | solution.py:190
  106.4 1.4 %middle_update.1 = (f32[256,1024]{1,0:T(8,128)S(1)}, f32[256,768]{1,0:T(8,128)S(1)}, f32[24,1,768]{2,1,0:T(1,128)S(1)}) custom-call(f32[24,1,768]{2,1,0:T(1,128)S(1)} %all_to_all.20.refs_0_, f32[24,768]{1,0:T(8,128)S(1)} %reshape.72.same_ref.refs_1_, f32[24,768]{1,0:T(8,128)S(1)} %reshape.75.swap_ref.refs_2_, f32[256,768]{1,0:T(8,128)S(1)} %get-tuple-element.11.refs_3_, ...), custom_call_target="tpu_custom_call" | custom-call | flops 805306368 | bytes 5242880 | tf_op jit(solution)/shard_map/middle_update/pallas_call | solution.py:271
  107.8 14.0 %all_to_all.21.refs_0_ = f32[24,1,768]{2,1,0:T(1,128)S(1)} all-to-all(f32[24,1,768]{2,1,0:T(1,128)S(1)} %get-tuple-element.13), channel_id=1, replica_groups=mesh['z'=12,'core'=2,'y'=8,'x'=4] {'z','core'}, dimensions={0} | all-to-all | bytes 147456 | tf_op jit(solution)/shard_map/last_stats_out/all_to_all | solution.py:190
  121.8 1.7 %last_update.1 = (f32[256,1024]{1,0:T(8,128)}, f32[1,256]{1,0:T(1,128)}) custom-call(f32[24,1,768]{2,1,0:T(1,128)S(1)} %all_to_all.21.refs_0_, f32[24,768]{1,0:T(8,128)S(1)} %reshape.72.same_ref.refs_1_, f32[24,768]{1,0:T(8,128)S(1)} %reshape.75.swap_ref.refs_2_, f32[256,768]{1,0:T(8,128)S(1)} %get-tuple-element.14.refs_3_, ...), custom_call_target="tpu_custom_call" | custom-call | flops 402653184 | bytes 5242880 | tf_op jit(solution)/shard_map/last_update/pallas_call | solution.py:281
  (10 shorter events, 0.1 us)
Async XLA Ops:
  2.3 26.6 %all-to-all-start.1 = ((bf16[24,2,384]{2,1,0:T(2,128)(2,1)}), bf16[24,2,384]{2,1,0:T(2,128)(2,1)S(1)}, u32[]{:S(2)}, u32[]{:S(2)}) async-start(bf16[24,2,384]{2,1,0:T(2,128)(2,1)} %sums_and_lists.1), calls=%async_computation.1 | async-start | bytes 73728 | tf_op jit(solution)/shard_map/sums_and_lists/all_to_all | solution.py:190
  28.8 4.4 %copy-start.1 = (s32[1,24]{1,0:T(1,128)S(1)}, s32[1,24]{1,0:T(1,128)}, u32[]{:S(2)}) copy-start(s32[1,24]{1,0:T(1,128)} %refs_1_.2) | copy-start | bytes 292
  28.8 60.7 %all-to-all-start = ((bf16[24,32,1024]{2,1,0:T(8,128)(2,1)}), bf16[24,32,1024]{2,1,0:T(8,128)(2,1)S(1)}, u32[]{:S(2)}, u32[]{:S(2)}) async-start(bf16[24,32,1024]{2,1,0:T(8,128)(2,1)} %bitcast.21), calls=%async_computation | async-start | bytes 3145728 | tf_op jit(solution)/shard_map/slabs_out/all_to_all | solution.py:190
  34.1 55.5 %copy-start = (bf16[1,1,256,1024]{3,2,1,0:T(8,128)(2,1)S(1)}, bf16[1,1,256,1024]{3,2,1,0:T(8,128)(2,1)}, u32[]{:S(2)}) copy-start(bf16[1,1,256,1024]{3,2,1,0:T(8,128)(2,1)} %param.7) | copy-start | bytes 1572868

commit v6 on v5

--- a/solution.py
+++ b/solution.py
@@ -9,7 +9,9 @@
 from jax.sharding import Mesh, PartitionSpec as P
 
 ITERS = 2
-DP = ("z", "core")
+DP = ("high", "low", "core")
+PEERS = ("low", "core", "high")
+LOW = 4
 LANES = 128
 
 prior_count = 1.0
@@ -28,6 +30,12 @@
         compiler_params=pltpu.CompilerParams(vmem_limit_bytes=16 * 2**20),
         cost_estimate=pl.CostEstimate(flops=flops, bytes_accessed=moved, transcendentals=0),
     )
+
+
+def peer_of(position, peers, cores):
+    high = peers // (cores * LOW)
+    chip, core = position // cores, position % cores
+    return (chip % LOW * cores + core) * high + chip // LOW
 
 
 def share_body(cores, lists_ref, emb_ref, out_ref):
@@ -45,11 +53,11 @@
         upper = jnp.concatenate([squares[:, at : at + part], names], axis=1)
         lower = jnp.concatenate([squares[:, at + part : at + 2 * part], names], axis=1)
         payload = jnp.concatenate([upper, lower], axis=0).astype(jnp.bfloat16)
-        for p in range(core, out_ref.shape[0], cores):
-            out_ref[p] = payload
-
-
-def dispatch(slab_rows, most, peers, lists_ref, home_ref, emb_ref, out_ref, table):
+        for position in range(core, out_ref.shape[0], cores):
+            out_ref[peer_of(position, out_ref.shape[0], cores)] = payload
+
+
+def dispatch(slab_rows, most, peers, cores, lists_ref, home_ref, emb_ref, out_ref, table):
     listed, slabs = lists_ref.shape
 
     def clear(p, carry):
@@ -66,7 +74,7 @@
 
     def place(n, carry):
         slab, k = n // listed, n % listed
-        p = home_ref[0, lists_ref[k, slab]]
+        p = peer_of(home_ref[0, lists_ref[k, slab]], peers, cores)
         seen = table[peers * most + p]
         table[p * most + jnp.minimum(seen, most - 1)] = slab
         table[peers * most + p] = seen + 1
@@ -187,7 +195,7 @@
 
 
 def spread(x):
-    return lax.all_to_all(x, DP, split_axis=0, concat_axis=0, tiled=True)
+    return lax.all_to_all(x, PEERS, split_axis=0, concat_axis=0, tiled=True)
 
 
 def per_device(embeddings, coarse_lists, home, centroids):
@@ -197,7 +205,7 @@
     slabs, listed = coarse_lists.shape
     slab_rows = row_count // slabs
     most = 2
-    cores = lax.axis_size(DP[1])
+    cores = lax.axis_size(DP[-1])
     part = width // (2 * cores)
     slots = peers * most * slab_rows
     f32 = jnp.float32
@@ -214,7 +222,7 @@
 
     with jax.named_scope("slabs_out"):
         outgoing = pl.pallas_call(
-            lambda *refs: dispatch(slab_rows, most, peers, *refs),
+            lambda *refs: dispatch(slab_rows, most, peers, cores, *refs),
             out_shape=jax.ShapeDtypeStruct((slots, width), jnp.bfloat16),
             in_specs=[pl.BlockSpec(memory_space=pltpu.SMEM)] * 2 + vmem(1),
             out_specs=vmem(1)[0],
@@ -225,14 +233,14 @@
     with jax.named_scope("feature_scale"):
         total = jnp.sum(shared[:, :, :part].astype(f32), axis=0).reshape(-1, LANES)
         total = lax.psum(lax.psum(total, "x"), "y")
-        total = lax.all_gather(total, DP[1], tiled=True)
+        total = lax.all_gather(total, DP[-1], tiled=True)
         scale = lax.rsqrt(total / total_rows + 1e-06)
 
     with jax.named_scope("slot_masks"):
-        me = lax.axis_index(DP)
+        me = lax.axis_index(PEERS)
         ids = jnp.arange(peers, dtype=jnp.int32)
         lists_all = shared[:, 0, part : part + slabs * listed].astype(jnp.int32)
-        home_of = jnp.sum(jnp.where(lists_all[:, :, None] == ids, home[0], 0), axis=2)
+        home_of = jnp.sum(jnp.where(lists_all[:, :, None] == ids, peer_of(home[0], peers, cores), 0), axis=2)
         hits = jnp.any(home_of.reshape(peers, slabs, listed)[..., None] == ids, axis=2)
         order = jnp.arange(slabs)
         earlier = (order[None, :] < order[:, None])[None, :, :, None]
@@ -290,8 +298,9 @@
 
 def solution(mesh):
     chips, rows = 12, 8
-    grid = np.asarray(mesh.devices).reshape(chips, mesh.devices.shape[0] // chips, rows, -1)
-    fine = Mesh(grid, ("z", "core", "y", "x"))
+    cores = mesh.devices.shape[0] // chips
+    grid = np.asarray(mesh.devices).reshape(chips // LOW, LOW, cores, rows, -1)
+    fine = Mesh(grid, (*DP, "y", "x"))
     group = ("y", "x")
     return jax.shard_map(
         per_device,

time: 124 us -> 124 us (level)
  waiting for transfers between devices: 29.9 us -> 26.1 us
  blocking collectives: 59.8 us -> 63.3 us
    all_to_all x2, waiting for transfers between devices: 29.9 us -> 26.1 us  [spread(): return lax.all_to_all(x, PEERS, split_axis=0, concat_axis=0, tiled=True)]
    all_to_all x2, blocking collectives: 29.9 us -> 33.4 us  [spread(): return lax.all_to_all(x, PEERS, split_axis=0, concat_axis=0, tiled=True)]
where the time goes in v6:
time: 124 us
  blocking collectives  63.3 us (51%)
  waiting for transfers between devices  26.1 us (21%)
  starting transfers between devices  20.8 us (17%)
  Pallas kernels  9.74 us (8%)
  other arithmetic  1.55 us (1%)
  local copies, waits for them, and re-layouts  1.26 us (1%)
    all_to_all x2, blocking collectives, spread(): return lax.all_to_all(x, PEERS, split_axis=0, concat_axis=0, tiled=True)  33.4 us
    all_to_all x2, waiting for transfers between devices, spread(): return lax.all_to_all(x, PEERS, split_axis=0, concat_axis=0, tiled=True)  26.1 us
    psum x2, blocking collectives, per_device(): total = lax.psum(lax.psum(total, 'x'), 'y')  23.8 us
    all_to_all x2, starting transfers between devices, spread(): return lax.all_to_all(x, PEERS, split_axis=0, concat_axis=0, tiled=True)  20.8 us
    all_gather x1, blocking collectives, per_device(): total = lax.all_gather(total, DP[-1], tiled=True)  6.04 us
    pallas_call x1, Pallas kernels, per_device(): pl.pallas_call(lambda *refs: dispatch(slab_rows, most, peers, cores, *ref...  4.11 us
  transfers between devices with their start and end apart: 2, of which 2 were waited for; matrix products, arithmetic and copies ran while one was open for 2% of the time, Pallas kernels for 3%

profile of v6, /device:TPU:1, one launch (start us, length us, event | category | flops | bytes accessed | tf_op | source)
XLA Modules:
  0.0 123.6 jit_solution(15107007946035874324)
XLA Ops:
  0.6 1.6 %sums_and_lists.1 = bf16[24,2,384]{2,1,0:T(2,128)(2,1)} custom-call(s32[4,8]{1,0:T(4,128)} %bitcast.38, bf16[128,1024]{1,0:T(8,128)(2,1)} %refs_1_.3), custom_call_target="tpu_custom_call" | custom-call | tf_op jit(solution)/shard_map/sums_and_lists/pallas_call | solution.py:215
  2.3 16.7 %all-to-all-start.1 = ((bf16[24,2,384]{2,1,0:T(2,128)(2,1)}), bf16[24,2,384]{2,1,0:T(2,128)(2,1)S(1)}, u32[]{:S(2)}, u32[]{:S(2)}) async-start(bf16[24,2,384]{2,1,0:T(2,128)(2,1)} %sums_and_lists.1), calls=%async_computation.1 | async-start | bytes 73728 | tf_op jit(solution)/shard_map/sums_and_lists/all_to_all | solution.py:198
  19.0 4.1 %slabs_out.1 = bf16[768,1024]{1,0:T(8,128)(2,1)} custom-call(s32[4,8]{1,0:T(4,128)} %bitcast.39, s32[1,24]{1,0:T(1,128)} %refs_1_.2, bf16[128,1024]{1,0:T(8,128)(2,1)} %refs_1_.3), custom_call_target="tpu_custom_call" | custom-call | tf_op jit(solution)/shard_map/slabs_out/pallas_call | solution.py:224
  23.1 5.7 %all-to-all-done.1 = bf16[24,2,384]{2,1,0:T(2,128)(2,1)S(1)} async-done(((bf16[24,2,384]{2,1,0:T(2,128)(2,1)}), bf16[24,2,384]{2,1,0:T(2,128)(2,1)S(1)}, u32[]{:S(2)}, u32[]{:S(2)}) %all-to-all-start.1) | async-done | bytes 36896 | tf_op jit(solution)/shard_map/sums_and_lists/all_to_all | solution.py:198
  28.8 0.0 copy-start.1
  28.8 4.1 %all-to-all-start = ((bf16[24,32,1024]{2,1,0:T(8,128)(2,1)}), bf16[24,32,1024]{2,1,0:T(8,128)(2,1)S(1)}, u32[]{:S(2)}, u32[]{:S(2)}) async-start(bf16[24,32,1024]{2,1,0:T(8,128)(2,1)} %bitcast.33), calls=%async_computation | async-start | bytes 3145728 | tf_op jit(solution)/shard_map/slabs_out/all_to_all | solution.py:198
  32.9 0.0 copy-done.1
  33.1 0.1 select_reduce_fusion.1
  33.2 0.1 copy.12
  33.3 0.1 copy.13
  33.4 0.2 fusion
  33.5 0.4 select_reduce_fusion
  33.9 0.0 copy-start
  33.9 0.5 select_reduce_fusion.2
  34.4 0.3 and_reduce_fusion
  34.7 0.1 copy.15
  34.8 0.1 copy.14
  34.9 0.2 broadcast_in_dim.62
  35.1 0.3 reshape.72.same_ref.refs_1_
  35.4 0.2 broadcast_in_dim.63
  35.6 0.3 reshape.75.swap_ref.refs_2_
  35.8 9.1 %psum.14 = f32[4,128]{1,0:T(4,128)S(1)} all-reduce(f32[4,128]{1,0:T(4,128)S(1)} %reshape.69), channel_id=1, replica_groups=mesh['high'=3,'low'=4,'core'=2,'y'=8,'x'=4] {'x'}, use_global_device_ids=true, to_apply=%region_1.0 | all-reduce | flops 512 | bytes 4096 | tf_op jit(solution)/shard_map/feature_scale/psum | solution.py:235
  44.9 14.7 %psum.15 = f32[4,128]{1,0:T(4,128)S(1)} all-reduce(f32[4,128]{1,0:T(4,128)S(1)} %psum.14), channel_id=1, replica_groups=mesh['high'=3,'low'=4,'core'=2,'y'=8,'x'=4] {'y'}, use_global_device_ids=true, to_apply=%region_2.0 | all-reduce | flops 512 | bytes 4096 | tf_op jit(solution)/shard_map/feature_scale/psum | solution.py:235
  59.6 6.0 %all-gather = f32[2,4,128]{2,1,0:T(4,128)S(1)} all-gather(f32[1,4,128]{2,1,0:T(4,128)S(1)} %bitcast.40), channel_id=1, replica_groups=mesh['high'=3,'low'=4,'core'=2,'y'=8,'x'=4] {'core'}, dimensions={0}, use_global_device_ids=true | all-gather | bytes 6144 | tf_op jit(solution)/shard_map/feature_scale/all_gather | solution.py:236
  65.7 20.4 %all-to-all-done = bf16[24,32,1024]{2,1,0:T(8,128)(2,1)S(1)} async-done(((bf16[24,32,1024]{2,1,0:T(8,128)(2,1)}), bf16[24,32,1024]{2,1,0:T(8,128)(2,1)S(1)}, u32[]{:S(2)}, u32[]{:S(2)}) %all-to-all-start) | async-done | bytes 1572896 | tf_op jit(solution)/shard_map/slabs_out/all_to_all | solution.py:198
  86.1 0.0 copy-done
  86.1 0.9 first_logits.1
  87.0 19.3 %all_to_all.20.refs_0_ = f32[24,1,768]{2,1,0:T(1,128)S(1)} all-to-all(f32[24,1,768]{2,1,0:T(1,128)S(1)} %get-tuple-element.10), channel_id=1, replica_groups=mesh['high'=3,'low'=4,'core'=2,'y'=8,'x'=4] {'low','core','high'}, dimensions={0} | all-to-all | bytes 147456 | tf_op jit(solution)/shard_map/stats_out/all_to_all | solution.py:198
  106.4 1.4 %middle_update.1 = (f32[256,1024]{1,0:T(8,128)S(1)}, f32[256,768]{1,0:T(8,128)S(1)}, f32[24,1,768]{2,1,0:T(1,128)S(1)}) custom-call(f32[24,1,768]{2,1,0:T(1,128)S(1)} %all_to_all.20.refs_0_, f32[24,768]{1,0:T(8,128)S(1)} %reshape.72.same_ref.refs_1_, f32[24,768]{1,0:T(8,128)S(1)} %reshape.75.swap_ref.refs_2_, f32[256,768]{1,0:T(8,128)S(1)} %get-tuple-element.11.refs_3_, ...), custom_call_target="tpu_custom_call" | custom-call | flops 805306368 | bytes 5242880 | tf_op jit(solution)/shard_map/middle_update/pallas_call | solution.py:279
  107.8 14.1 %all_to_all.21.refs_0_ = f32[24,1,768]{2,1,0:T(1,128)S(1)} all-to-all(f32[24,1,768]{2,1,0:T(1,128)S(1)} %get-tuple-element.13), channel_id=1, replica_groups=mesh['high'=3,'low'=4,'core'=2,'y'=8,'x'=4] {'low','core','high'}, dimensions={0} | all-to-all | bytes 147456 | tf_op jit(solution)/shard_map/last_stats_out/all_to_all | solution.py:198
  121.9 1.7 %last_update.1 = (f32[256,1024]{1,0:T(8,128)}, f32[1,256]{1,0:T(1,128)}) custom-call(f32[24,1,768]{2,1,0:T(1,128)S(1)} %all_to_all.21.refs_0_, f32[24,768]{1,0:T(8,128)S(1)} %reshape.72.same_ref.refs_1_, f32[24,768]{1,0:T(8,128)S(1)} %reshape.75.swap_ref.refs_2_, f32[256,768]{1,0:T(8,128)S(1)} %get-tuple-element.14.refs_3_, ...), custom_call_target="tpu_custom_call" | custom-call | flops 402653184 | bytes 5242880 | tf_op jit(solution)/shard_map/last_update/pallas_call | solution.py:289
  (11 shorter events, 0.2 us)
Async XLA Ops:
  2.3 26.5 %all-to-all-start.1 = ((bf16[24,2,384]{2,1,0:T(2,128)(2,1)}), bf16[24,2,384]{2,1,0:T(2,128)(2,1)S(1)}, u32[]{:S(2)}, u32[]{:S(2)}) async-start(bf16[24,2,384]{2,1,0:T(2,128)(2,1)} %sums_and_lists.1), calls=%async_computation.1 | async-start | bytes 73728 | tf_op jit(solution)/shard_map/sums_and_lists/all_to_all | solution.py:198
  28.8 4.2 %copy-start.1 = (s32[1,24]{1,0:T(1,128)S(1)}, s32[1,24]{1,0:T(1,128)}, u32[]{:S(2)}) copy-start(s32[1,24]{1,0:T(1,128)} %refs_1_.2) | copy-start | bytes 292
  28.8 57.3 %all-to-all-start = ((bf16[24,32,1024]{2,1,0:T(8,128)(2,1)}), bf16[24,32,1024]{2,1,0:T(8,128)(2,1)S(1)}, u32[]{:S(2)}, u32[]{:S(2)}) async-start(bf16[24,32,1024]{2,1,0:T(8,128)(2,1)} %bitcast.33), calls=%async_computation | async-start | bytes 3145728 | tf_op jit(solution)/shard_map/slabs_out/all_to_all | solution.py:198
  33.9 52.2 %copy-start = (bf16[1,1,256,1024]{3,2,1,0:T(8,128)(2,1)S(1)}, bf16[1,1,256,1024]{3,2,1,0:T(8,128)(2,1)}, u32[]{:S(2)}) copy-start(bf16[1,1,256,1024]{3,2,1,0:T(8,128)(2,1)} %param.7) | copy-start | bytes 1572868

commit v7 on v5

--- a/solution.py
+++ b/solution.py
@@ -10,6 +10,7 @@
 
 ITERS = 2
 DP = ("z", "core")
+PEERS = ("core", "z")
 LANES = 128
 
 prior_count = 1.0
@@ -28,6 +29,10 @@
         compiler_params=pltpu.CompilerParams(vmem_limit_bytes=16 * 2**20),
         cost_estimate=pl.CostEstimate(flops=flops, bytes_accessed=moved, transcendentals=0),
     )
+
+
+def peer_of(position, peers, cores):
+    return (position % cores) * (peers // cores) + position // cores
 
 
 def share_body(cores, lists_ref, emb_ref, out_ref):
@@ -45,11 +50,11 @@
         upper = jnp.concatenate([squares[:, at : at + part], names], axis=1)
         lower = jnp.concatenate([squares[:, at + part : at + 2 * part], names], axis=1)
         payload = jnp.concatenate([upper, lower], axis=0).astype(jnp.bfloat16)
-        for p in range(core, out_ref.shape[0], cores):
-            out_ref[p] = payload
-
-
-def dispatch(slab_rows, most, peers, lists_ref, home_ref, emb_ref, out_ref, table):
+        for p in range(out_ref.shape[0] // cores):
+            out_ref[core * (out_ref.shape[0] // cores) + p] = payload
+
+
+def dispatch(slab_rows, most, peers, cores, lists_ref, home_ref, emb_ref, out_ref, table):
     listed, slabs = lists_ref.shape
 
     def clear(p, carry):
@@ -66,7 +71,7 @@
 
     def place(n, carry):
         slab, k = n // listed, n % listed
-        p = home_ref[0, lists_ref[k, slab]]
+        p = peer_of(home_ref[0, lists_ref[k, slab]], peers, cores)
         seen = table[peers * most + p]
         table[p * most + jnp.minimum(seen, most - 1)] = slab
         table[peers * most + p] = seen + 1
@@ -187,7 +192,7 @@
 
 
 def spread(x):
-    return lax.all_to_all(x, DP, split_axis=0, concat_axis=0, tiled=True)
+    return lax.all_to_all(x, PEERS, split_axis=0, concat_axis=0, tiled=True)
 
 
 def per_device(embeddings, coarse_lists, home, centroids):
@@ -214,7 +219,7 @@
 
     with jax.named_scope("slabs_out"):
         outgoing = pl.pallas_call(
-            lambda *refs: dispatch(slab_rows, most, peers, *refs),
+            lambda *refs: dispatch(slab_rows, most, peers, cores, *refs),
             out_shape=jax.ShapeDtypeStruct((slots, width), jnp.bfloat16),
             in_specs=[pl.BlockSpec(memory_space=pltpu.SMEM)] * 2 + vmem(1),
             out_specs=vmem(1)[0],
@@ -229,10 +234,10 @@
         scale = lax.rsqrt(total / total_rows + 1e-06)
 
     with jax.named_scope("slot_masks"):
-        me = lax.axis_index(DP)
+        me = lax.axis_index(PEERS)
         ids = jnp.arange(peers, dtype=jnp.int32)
         lists_all = shared[:, 0, part : part + slabs * listed].astype(jnp.int32)
-        home_of = jnp.sum(jnp.where(lists_all[:, :, None] == ids, home[0], 0), axis=2)
+        home_of = jnp.sum(jnp.where(lists_all[:, :, None] == ids, peer_of(home[0], peers, cores), 0), axis=2)
         hits = jnp.any(home_of.reshape(peers, slabs, listed)[..., None] == ids, axis=2)
         order = jnp.arange(slabs)
         earlier = (order[None, :] < order[:, None])[None, :, :, None]

time: 124 us -> 124 us (level)
  waiting for transfers between devices: 29.9 us -> 27.8 us
  blocking collectives: 59.8 us -> 61.3 us
    all_to_all x2, waiting for transfers between devices: 29.9 us -> 27.8 us  [spread(): return lax.all_to_all(x, PEERS, split_axis=0, concat_axis=0, tiled=True)]
    all_to_all x2, blocking collectives: 29.9 us -> 31.5 us  [spread(): return lax.all_to_all(x, PEERS, split_axis=0, concat_axis=0, tiled=True)]
where the time goes in v7:
time: 124 us; the launch traced here: 123 us
  blocking collectives  61.3 us (49%)
  waiting for transfers between devices  27.8 us (22%)
  starting transfers between devices  21.2 us (17%)
  Pallas kernels  9.52 us (8%)
  other arithmetic  1.54 us (1%)
  local copies, waits for them, and re-layouts  1.26 us (1%)
    all_to_all x2, blocking collectives, spread(): return lax.all_to_all(x, PEERS, split_axis=0, concat_axis=0, tiled=True)  31.5 us
    all_to_all x2, waiting for transfers between devices, spread(): return lax.all_to_all(x, PEERS, split_axis=0, concat_axis=0, tiled=True)  27.8 us
    psum x2, blocking collectives, per_device(): total = lax.psum(lax.psum(total, 'x'), 'y')  23.7 us
    all_to_all x2, starting transfers between devices, spread(): return lax.all_to_all(x, PEERS, split_axis=0, concat_axis=0, tiled=True)  21.2 us
    all_gather x1, blocking collectives, per_device(): total = lax.all_gather(total, DP[1], tiled=True)  6.08 us
    pallas_call x1, Pallas kernels, per_device(): pl.pallas_call(lambda *refs: dispatch(slab_rows, most, peers, cores, *ref...  3.89 us
  transfers between devices with their start and end apart: 2, of which 2 were waited for; matrix products, arithmetic and copies ran while one was open for 2% of the time, Pallas kernels for 3%

profile of v7, /device:TPU:1, one launch (start us, length us, event | category | flops | bytes accessed | tf_op | source)
XLA Modules:
  0.0 123.4 jit_solution(15904232057681808506)
XLA Ops:
  0.6 1.6 %sums_and_lists.1 = bf16[24,2,384]{2,1,0:T(2,128)(2,1)} custom-call(s32[4,8]{1,0:T(4,128)} %bitcast.38, bf16[128,1024]{1,0:T(8,128)(2,1)} %refs_1_.3), custom_call_target="tpu_custom_call" | custom-call | tf_op jit(solution)/shard_map/sums_and_lists/pallas_call | solution.py:212
  2.3 16.7 %all-to-all-start.1 = ((bf16[24,2,384]{2,1,0:T(2,128)(2,1)}), bf16[24,2,384]{2,1,0:T(2,128)(2,1)S(1)}, u32[]{:S(2)}, u32[]{:S(2)}) async-start(bf16[24,2,384]{2,1,0:T(2,128)(2,1)} %sums_and_lists.1), calls=%async_computation.1 | async-start | bytes 73728 | tf_op jit(solution)/shard_map/sums_and_lists/all_to_all | solution.py:195
  19.0 3.9 %slabs_out.1 = bf16[768,1024]{1,0:T(8,128)(2,1)} custom-call(s32[4,8]{1,0:T(4,128)} %bitcast.39, s32[1,24]{1,0:T(1,128)} %refs_1_.2, bf16[128,1024]{1,0:T(8,128)(2,1)} %refs_1_.3), custom_call_target="tpu_custom_call" | custom-call | tf_op jit(solution)/shard_map/slabs_out/pallas_call | solution.py:221
  22.9 6.0 %all-to-all-done.1 = bf16[24,2,384]{2,1,0:T(2,128)(2,1)S(1)} async-done(((bf16[24,2,384]{2,1,0:T(2,128)(2,1)}), bf16[24,2,384]{2,1,0:T(2,128)(2,1)S(1)}, u32[]{:S(2)}, u32[]{:S(2)}) %all-to-all-start.1) | async-done | bytes 36896 | tf_op jit(solution)/shard_map/sums_and_lists/all_to_all | solution.py:195
  28.8 0.0 copy-start.1
  28.8 4.5 %all-to-all-start = ((bf16[24,32,1024]{2,1,0:T(8,128)(2,1)}), bf16[24,32,1024]{2,1,0:T(8,128)(2,1)S(1)}, u32[]{:S(2)}, u32[]{:S(2)}) async-start(bf16[24,32,1024]{2,1,0:T(8,128)(2,1)} %bitcast.33), calls=%async_computation | async-start | bytes 3145728 | tf_op jit(solution)/shard_map/slabs_out/all_to_all | solution.py:195
  33.4 0.0 copy-done.1
  33.5 0.1 select_reduce_fusion.1
  33.6 0.1 copy.12
  33.7 0.1 copy.13
  33.8 0.2 fusion
  34.0 0.4 select_reduce_fusion
  34.3 0.0 copy-start
  34.3 0.5 select_reduce_fusion.2
  34.9 0.3 and_reduce_fusion
  35.1 0.1 copy.15
  35.2 0.1 copy.14
  35.3 0.2 broadcast_in_dim.62
  35.5 0.3 reshape.72.same_ref.refs_1_
  35.8 0.2 broadcast_in_dim.63
  36.0 0.3 reshape.75.swap_ref.refs_2_
  36.3 8.8 %psum.14 = f32[4,128]{1,0:T(4,128)S(1)} all-reduce(f32[4,128]{1,0:T(4,128)S(1)} %reshape.69), channel_id=1, replica_groups=mesh['z'=12,'core'=2,'y'=8,'x'=4] {'x'}, use_global_device_ids=true, to_apply=%region_1.0 | all-reduce | flops 512 | bytes 4096 | tf_op jit(solution)/shard_map/feature_scale/psum | solution.py:232
  45.0 14.9 %psum.15 = f32[4,128]{1,0:T(4,128)S(1)} all-reduce(f32[4,128]{1,0:T(4,128)S(1)} %psum.14), channel_id=1, replica_groups=mesh['z'=12,'core'=2,'y'=8,'x'=4] {'y'}, use_global_device_ids=true, to_apply=%region_2.0 | all-reduce | flops 512 | bytes 4096 | tf_op jit(solution)/shard_map/feature_scale/psum | solution.py:232
  60.0 6.1 %all-gather = f32[2,4,128]{2,1,0:T(4,128)S(1)} all-gather(f32[1,4,128]{2,1,0:T(4,128)S(1)} %bitcast.40), channel_id=1, replica_groups=mesh['z'=12,'core'=2,'y'=8,'x'=4] {'core'}, dimensions={0}, use_global_device_ids=true | all-gather | bytes 6144 | tf_op jit(solution)/shard_map/feature_scale/all_gather | solution.py:233
  66.0 21.9 %all-to-all-done = bf16[24,32,1024]{2,1,0:T(8,128)(2,1)S(1)} async-done(((bf16[24,32,1024]{2,1,0:T(8,128)(2,1)}), bf16[24,32,1024]{2,1,0:T(8,128)(2,1)S(1)}, u32[]{:S(2)}, u32[]{:S(2)}) %all-to-all-start) | async-done | bytes 1572896 | tf_op jit(solution)/shard_map/slabs_out/all_to_all | solution.py:195
  87.9 0.0 copy-done
  87.9 0.9 first_logits.1
  88.8 17.3 %all_to_all.20.refs_0_ = f32[24,1,768]{2,1,0:T(1,128)S(1)} all-to-all(f32[24,1,768]{2,1,0:T(1,128)S(1)} %get-tuple-element.10), channel_id=1, replica_groups=mesh['z'=12,'core'=2,'y'=8,'x'=4] {'core','z'}, dimensions={0} | all-to-all | bytes 147456 | tf_op jit(solution)/shard_map/stats_out/all_to_all | solution.py:195
  106.2 1.4 %middle_update.1 = (f32[256,1024]{1,0:T(8,128)S(1)}, f32[256,768]{1,0:T(8,128)S(1)}, f32[24,1,768]{2,1,0:T(1,128)S(1)}) custom-call(f32[24,1,768]{2,1,0:T(1,128)S(1)} %all_to_all.20.refs_0_, f32[24,768]{1,0:T(8,128)S(1)} %reshape.72.same_ref.refs_1_, f32[24,768]{1,0:T(8,128)S(1)} %reshape.75.swap_ref.refs_2_, f32[256,768]{1,0:T(8,128)S(1)} %get-tuple-element.11.refs_3_, ...), custom_call_target="tpu_custom_call" | custom-call | flops 805306368 | bytes 5242880 | tf_op jit(solution)/shard_map/middle_update/pallas_call | solution.py:276
  107.5 14.2 %all_to_all.21.refs_0_ = f32[24,1,768]{2,1,0:T(1,128)S(1)} all-to-all(f32[24,1,768]{2,1,0:T(1,128)S(1)} %get-tuple-element.13), channel_id=1, replica_groups=mesh['z'=12,'core'=2,'y'=8,'x'=4] {'core','z'}, dimensions={0} | all-to-all | bytes 147456 | tf_op jit(solution)/shard_map/last_stats_out/all_to_all | solution.py:195
  121.7 1.7 %last_update.1 = (f32[256,1024]{1,0:T(8,128)}, f32[1,256]{1,0:T(1,128)}) custom-call(f32[24,1,768]{2,1,0:T(1,128)S(1)} %all_to_all.21.refs_0_, f32[24,768]{1,0:T(8,128)S(1)} %reshape.72.same_ref.refs_1_, f32[24,768]{1,0:T(8,128)S(1)} %reshape.75.swap_ref.refs_2_, f32[256,768]{1,0:T(8,128)S(1)} %get-tuple-element.14.refs_3_, ...), custom_call_target="tpu_custom_call" | custom-call | flops 402653184 | bytes 5242880 | tf_op jit(solution)/shard_map/last_update/pallas_call | solution.py:286
  (11 shorter events, 0.2 us)
Async XLA Ops:
  2.3 26.6 %all-to-all-start.1 = ((bf16[24,2,384]{2,1,0:T(2,128)(2,1)}), bf16[24,2,384]{2,1,0:T(2,128)(2,1)S(1)}, u32[]{:S(2)}, u32[]{:S(2)}) async-start(bf16[24,2,384]{2,1,0:T(2,128)(2,1)} %sums_and_lists.1), calls=%async_computation.1 | async-start | bytes 73728 | tf_op jit(solution)/shard_map/sums_and_lists/all_to_all | solution.py:195
  28.8 4.6 %copy-start.1 = (s32[1,24]{1,0:T(1,128)S(1)}, s32[1,24]{1,0:T(1,128)}, u32[]{:S(2)}) copy-start(s32[1,24]{1,0:T(1,128)} %refs_1_.2) | copy-start | bytes 292
  28.8 59.1 %all-to-all-start = ((bf16[24,32,1024]{2,1,0:T(8,128)(2,1)}), bf16[24,32,1024]{2,1,0:T(8,128)(2,1)S(1)}, u32[]{:S(2)}, u32[]{:S(2)}) async-start(bf16[24,32,1024]{2,1,0:T(8,128)(2,1)} %bitcast.33), calls=%async_computation | async-start | bytes 3145728 | tf_op jit(solution)/shard_map/slabs_out/all_to_all | solution.py:195
  34.3 53.6 %copy-start = (bf16[1,1,256,1024]{3,2,1,0:T(8,128)(2,1)S(1)}, bf16[1,1,256,1024]{3,2,1,0:T(8,128)(2,1)}, u32[]{:S(2)}) copy-start(bf16[1,1,256,1024]{3,2,1,0:T(8,128)(2,1)} %param.7) | copy-start | bytes 1572868
